TPU v7x, 256 devices: a whole 4x4x8 slice. The times are simulated.
256 devices in a mesh: dp: 2 (over y_hi), row: 8 (over z), col: 16 (over x, y_lo, core).
Axes of the slice: x: 4, y: 4 (y_hi: 2, y_lo: 2; y = y_hi * 2 + y_lo), z: 8, core: 2. Of those that a mesh axis runs over, the one named last changes fastest.
Arguments:
- out_grads: bfloat16 [512, 28672], P('row', ('dp', 'col')), may hold values from -6 to 6
- layer_inputs: bfloat16 [512, 8192], P('col', ('dp', 'row')), may hold values from -6 to 6
- basis_output: bfloat16 [28672, 28672], P(('dp', 'col'), 'row'), may hold values from -0.03125 to 0.03125
- basis_input: bfloat16 [8192, 8192], P(('dp', 'row'), 'col'), may hold values from -0.0625 to 0.0625
- eigenvalues: bfloat16 [28672, 8192], P('row', 'col'), may hold values from 0.0009 to 405
- query_left: bfloat16 [28672, 128], P(('dp', 'col')), may hold values from -0.03125 to 0.03125
- query_right: bfloat16 [8192, 128], P(('dp', 'row')), may hold values from -0.01171875 to 0.01171875
Outputs:
- influence: float32 [4, 512], P('dp')
All inputs are finite; a program needn't handle non-finite values.
Results may differ from a plain program's by a relative error of at most 0.005.
Values may be sent and summed in bfloat16 or wider, within the bound.
A program may use at most 64 MiB of HBM per device.

v0:
```python
import jax
import jax.numpy as jnp
from jax import lax
from jax.sharding import Mesh
from jax.sharding import PartitionSpec as P

DG = 28672
DA = 8192
RANK = 32
COL = ("col_0", "col_1", "col_2")
ROW_COL = ("row", "col_0", "col_1", "col_2")
DP_COL = ("dp", "col_0", "col_1", "col_2")


DAMP_RATIO = 0.1


def copy_for_each(shard, axis):
    copies = jnp.broadcast_to(shard, (lax.axis_size(axis), *shard.shape))
    return lax.all_to_all(copies, axis, split_axis=0, concat_axis=0, tiled=True)


def in_order(tiles, dim):
    lengths = list(tiles.shape[1:])
    lengths[dim] *= tiles.shape[0]
    return jnp.moveaxis(tiles, 0, dim).reshape(lengths)


def collect(shard, axis, dim):
    tiles = copy_for_each(shard, axis)
    return in_order(tiles, dim)


def by_axis(shard, axes):
    for axis in axes:
        shard = lax.psum(shard, axis)
    return shard


def cut_along(shard, dim, count):
    before, after = (shard.shape[:dim], shard.shape[dim + 1 :])
    return jnp.moveaxis(shard.reshape(*before, count, -1, *after), dim, 0)


def sent_and_summed(shard, axis, dim):
    count = lax.axis_size(axis)
    tiles = lax.all_to_all(cut_along(shard, dim, count), axis, 0, 0, tiled=True)
    return jnp.sum(tiles, axis=0)


def over_copies(shard, axis):
    return copy_for_each(shard, axis).sum(axis=0)


def score_block(rotated_grads, rotated_inputs, left_cols, right_cols, eigen_block, damping):
    query_count = left_cols.shape[1] // RANK
    inputs_wide = rotated_inputs.astype(jnp.float32)
    shifted = eigen_block.astype(jnp.float32) + damping
    results = []
    for query_index in range(query_count):
        left_rank = left_cols[:, query_index * RANK : (query_index + 1) * RANK]
        right_rank = right_cols[:, query_index * RANK : (query_index + 1) * RANK]
        product = jnp.einsum("kr,lr->kl", left_rank, right_rank, preferred_element_type=jnp.float32)
        precond = (product / shifted).astype(jnp.bfloat16)
        weighted = jnp.dot(rotated_grads, precond, preferred_element_type=jnp.float32)
        results.append(jnp.sum(weighted * inputs_wide, axis=1))
    return jnp.stack(results)


def local(out_grads, layer_inputs, basis_output, basis_input, eigenvalues, query_left, query_right):
    grad_part = jnp.dot(
        collect(out_grads, "row", 0), basis_output, preferred_element_type=jnp.float32
    )
    input_part = jnp.dot(
        collect(layer_inputs, COL, 0), basis_input, preferred_element_type=jnp.float32
    )
    left_part = jnp.einsum(
        "ik,ic->kc", basis_output, query_left, preferred_element_type=jnp.float32
    )
    right_part = jnp.einsum(
        "jl,jc->lc", basis_input, query_right, preferred_element_type=jnp.float32
    )
    eigen_total = by_axis(jnp.sum(eigenvalues.astype(jnp.float32)), ROW_COL)
    damping = DAMP_RATIO * eigen_total / (DG * DA)
    rotated_grads = lax.psum(grad_part, DP_COL).astype(jnp.bfloat16)
    rotated_inputs = lax.psum(input_part, ("dp", "row")).astype(jnp.bfloat16)
    left_cols = lax.psum(sent_and_summed(left_part, "dp", 1), COL).astype(jnp.bfloat16)
    right_cols = over_copies(sent_and_summed(right_part, "dp", 1), "row").astype(jnp.bfloat16)
    partial_value = score_block(
        rotated_grads, rotated_inputs, left_cols, right_cols, eigenvalues, damping
    )
    influence = by_axis(partial_value, ROW_COL)
    return influence


def solution(mesh):
    finer = Mesh(
        mesh.devices.reshape(mesh.shape["dp"], mesh.shape["row"], 4, 2, 2),
        ("dp", "row", "col_0", "col_1", "col_2"),
    )
    in_specs = (
        P("row", DP_COL),
        P(COL, ("dp", "row")),
        P(DP_COL, "row"),
        P(("dp", "row"), COL),
        P("row", COL),
        P(DP_COL, None),
        P(("dp", "row"), None),
    )
    out_specs = P("dp", None)
    return jax.shard_map(local, mesh=finer, in_specs=in_specs, out_specs=out_specs, check_vma=False)
```

profile of v0, /device:TPU:1, one launch (start us, length us, event | category | flops | bytes accessed | tf_op | source)
XLA Modules:
  0.0 475.7 jit_solution(6984877001439614228)
XLA Ops:
  0.0 0.0 copy-start
  0.0 1.0 copy-done
  1.0 1.2 fusion.30
  2.2 10.3 %all_to_all.25 = f32[2,512,64]{1,2,0:T(8,128)S(1)} all-to-all(f32[2,512,64]{1,2,0:T(8,128)S(1)} %bitcast.21), channel_id=1, replica_groups=mesh['dp'=2,'row'=8,'col_0'=4,'col_1'=2,'col_2'=2] {'dp'}, dimensions={0} | all-to-all | bytes 524288 | tf_op jit(solution)/shard_map/all_to_all | solution.py:47
  12.6 1.6 broadcast_in_dim.11
  14.2 6.5 %all-to-all-start.4 = ((bf16[16,32,512]{2,1,0:T(8,128)(2,1)}), bf16[16,32,512]{2,1,0:T(8,128)(2,1)S(1)}, u32[]{:S(2)}, u32[]{:S(2)}) async-start(bf16[16,32,512]{2,1,0:T(8,128)(2,1)} %broadcast_in_dim.11), calls=%async_computation.4 | async-start | bytes 1048576 | tf_op jit(solution)/shard_map/all_to_all | solution.py:20
  20.7 5.3 %fusion.29 = f32[3584,128]{0,1:T(8,128)} fusion(bf16[896,3584]{1,0:T(8,128)(2,1)} %param.9, bf16[896,128]{1,0:T(8,128)(2,1)} %param.12), kind=kOutput, calls=%fused_computation.20 | convolution fusion | flops 822083584 | bytes 8486912 | tf_op jit(solution)/shard_map/ik,ic->kc/dot_general | solution.py:77
  26.0 4.4 all-to-all-done.4
  30.3 0.0 copy-start.1
  30.3 3.7 all-to-all-start.1
  34.1 4.5 convert_reduce_fusion
  38.6 18.0 %psum.79 = f32[]{:T(128)} all-reduce(f32[]{:T(128)} %convert_reduce_fusion), channel_id=1, replica_groups=mesh['dp'=2,'row'=8,'col_0'=4,'col_1'=2,'col_2'=2] {'row'}, use_global_device_ids=true, to_apply=%region_6.0 | all-reduce | flops 1 | bytes 8 | tf_op jit(solution)/shard_map/psum | solution.py:36
  56.6 7.3 %psum.80 = f32[]{:T(128)} all-reduce(f32[]{:T(128)} %psum.79), channel_id=1, replica_groups=mesh['dp'=2,'row'=8,'col_0'=4,'col_1'=2,'col_2'=2] {'col_0'}, use_global_device_ids=true, to_apply=%region_7.0 | all-reduce | flops 1 | bytes 8 | tf_op jit(solution)/shard_map/psum | solution.py:36
  64.0 4.4 psum.81
  68.4 9.6 %psum.82 = f32[]{:T(128)} all-reduce(f32[]{:T(128)} %psum.81), channel_id=1, replica_groups=mesh['dp'=2,'row'=8,'col_0'=4,'col_1'=2,'col_2'=2] {'col_2'}, use_global_device_ids=true, to_apply=%region_9.0 | all-reduce | flops 1 | bytes 8 | tf_op jit(solution)/shard_map/psum | solution.py:36
  78.7 0.0 copy-done.1
  78.7 1.5 fusion.31
  80.2 0.0 all-to-all-done.1
  80.3 1.9 broadcast_in_dim.9
  82.2 4.2 all-to-all-start
  86.4 91.8 %all-reduce.5 = bf16[512,512]{0,1:T(8,128)(2,1)} all-reduce(f32[512,512]{0,1:T(8,128)S(1)} %fusion.31), channel_id=1, replica_groups=mesh['dp'=2,'row'=8,'col_0'=4,'col_1'=2,'col_2'=2] {'dp','row'}, use_global_device_ids=true, to_apply=%region_10.0 | all-reduce | flops 262144 | bytes 1572864 | tf_op jit(solution)/shard_map/psum | solution.py:86
  178.3 0.2 reduce_sum.54
  178.5 71.9 %all-reduce.4 = bf16[3584,64]{0,1:T(8,128)(2,1)} all-reduce(f32[3584,64]{0,1:T(8,128)S(1)} %reduce_sum.54), channel_id=1, replica_groups=mesh['dp'=2,'row'=8,'col_0'=4,'col_1'=2,'col_2'=2] {'col_0','col_1','col..., use_global_device_ids=true, to_apply=%region_2.0 | all-reduce | flops 229376 | bytes 1376256 | tf_op jit(solution)/shard_map/psum | solution.py:87
  250.3 0.0 all-to-all-done
  250.3 1.1 broadcast_in_dim.10
  251.4 3.6 all-to-all-start.3
  255.0 10.1 %fusion.28 = f32[512,3584]{1,0:T(8,128)} fusion(bf16[512,896]{1,0:T(8,128)(2,1)} %bitcast, bf16[896,3584]{1,0:T(8,128)(2,1)} %param.9), kind=kOutput, calls=%fused_computation.19 | convolution fusion | flops 3288334336 | bytes 14680064 | tf_op jit(solution)/shard_map/dot_general | solution.py:71
  265.1 0.0 copy-start.2
  265.1 0.0 copy-start.3
  265.1 165.6 %all-reduce.3 = bf16[512,3584]{1,0:T(8,128)(2,1)} all-reduce(f32[512,3584]{1,0:T(8,128)} %fusion.28), channel_id=1, replica_groups=mesh['dp'=2,'row'=8,'col_0'=4,'col_1'=2,'col_2'=2] {'dp','col_0','col_1'..., use_global_device_ids=true, to_apply=%region_0.0 | all-reduce | flops 1835008 | bytes 11010048 | tf_op jit(solution)/shard_map/psum | solution.py:85
  430.6 0.0 all-to-all-done.3
  430.6 0.1 reduce_sum.56
  430.7 0.0 copy-done.2
  430.7 0.0 copy-done.3
  430.7 6.6 %fusion.17 = f32[512]{0:T(512)S(1)} fusion(bf16[3584,512]{1,0:T(8,128)(2,1)} %param.11, f32[]{:T(128)S(6)} %div.9, bf16[512,3584]{1,0:T(8,128)(2,1)} %all-reduce.3, bf16[512,512]{0,1:T(8,128)(2,1)S(1)} %copy-done.2, bf16[3584,64]{0,1:T(8,128)(2,1)S(1)} %copy-done.3, bf16[512,64]{0,1:T(8,128)(2,1)S(1)} %reduce_sum.56), kind=kOutput, calls=%fused_computation.13 | convolution fusion | flops 2004614656 | bytes 8128516 | tf_op jit(solution)/shard_map/dot_general | solution.py:65
  437.4 6.6 %fusion.14 = f32[512]{0:T(512)S(1)} fusion(bf16[3584,512]{1,0:T(8,128)(2,1)} %param.11, f32[]{:T(128)S(6)} %div.9, bf16[512,3584]{1,0:T(8,128)(2,1)} %all-reduce.3, bf16[512,512]{0,1:T(8,128)(2,1)S(1)} %copy-done.2, bf16[3584,64]{0,1:T(8,128)(2,1)S(1)} %copy-done.3, bf16[512,64]{0,1:T(8,128)(2,1)S(1)} %reduce_sum.56), kind=kOutput, calls=%fused_computation.12 | convolution fusion | flops 2004614656 | bytes 8128516 | tf_op jit(solution)/shard_map/dot_general | solution.py:65
  444.0 13.6 %psum.84 = f32[2,512]{1,0:T(2,128)S(1)} all-reduce(f32[2,512]{1,0:T(2,128)S(1)} %pad_maximum_fusion), channel_id=1, replica_groups=mesh['dp'=2,'row'=8,'col_0'=4,'col_1'=2,'col_2'=2] {'row'}, use_global_device_ids=true, to_apply=%region_13.0 | all-reduce | flops 1024 | bytes 8192 | tf_op jit(solution)/shard_map/psum | solution.py:36
  457.6 6.0 %psum.85 = f32[2,512]{1,0:T(2,128)S(1)} all-reduce(f32[2,512]{1,0:T(2,128)S(1)} %psum.84), channel_id=1, replica_groups=mesh['dp'=2,'row'=8,'col_0'=4,'col_1'=2,'col_2'=2] {'col_0'}, use_global_device_ids=true, to_apply=%region_14.0 | all-reduce | flops 1024 | bytes 8192 | tf_op jit(solution)/shard_map/psum | solution.py:36
  463.6 4.1 psum.86
  467.6 8.1 %psum.87 = f32[2,512]{1,0:T(2,128)} all-reduce(f32[2,512]{1,0:T(2,128)S(1)} %psum.86), channel_id=1, replica_groups=mesh['dp'=2,'row'=8,'col_0'=4,'col_1'=2,'col_2'=2] {'col_2'}, use_global_device_ids=true, to_apply=%region_16.0 | all-reduce | flops 1024 | bytes 8192 | tf_op jit(solution)/shard_map/psum | solution.py:36
  (2 shorter events, 0.0 us)
Async XLA Ops:
  0.0 1.0 copy-start
  14.2 16.2 %all-to-all-start.4 = ((bf16[16,32,512]{2,1,0:T(8,128)(2,1)}), bf16[16,32,512]{2,1,0:T(8,128)(2,1)S(1)}, u32[]{:S(2)}, u32[]{:S(2)}) async-start(bf16[16,32,512]{2,1,0:T(8,128)(2,1)} %broadcast_in_dim.11), calls=%async_computation.4 | async-start | bytes 1048576 | tf_op jit(solution)/shard_map/all_to_all | solution.py:20
  30.3 48.4 %copy-start.1 = (bf16[16,32,512]{2,1,0:T(8,128)(2,1)}, bf16[16,32,512]{2,1,0:T(8,128)(2,1)S(1)}, u32[]{:S(2)}) copy-start(bf16[16,32,512]{2,1,0:T(8,128)(2,1)S(1)} %all-to-all-done.4) | copy-start | bytes 1572868
  30.3 49.9 %all-to-all-start.1 = ((f32[2,3584,64]{1,2,0:T(8,128)}), f32[2,3584,64]{1,2,0:T(8,128)S(1)}, u32[]{:S(2)}, u32[]{:S(2)}) async-start(f32[2,3584,64]{1,2,0:T(8,128)} %bitcast.2), calls=%async_computation.1 | async-start | bytes 3670016 | tf_op jit(solution)/shard_map/all_to_all | solution.py:47
  82.2 168.1 %all-to-all-start = ((bf16[8,64,896]{2,1,0:T(8,128)(2,1)}), bf16[8,64,896]{2,1,0:T(8,128)(2,1)}, u32[]{:S(2)}, u32[]{:S(2)}) async-start(bf16[8,64,896]{2,1,0:T(8,128)(2,1)} %broadcast_in_dim.9), calls=%async_computation | async-start | bytes 1835008 | tf_op jit(solution)/shard_map/all_to_all | solution.py:20
  251.4 179.2 %all-to-all-start.3 = ((f32[8,512,64]{1,2,0:T(8,128)}), f32[8,512,64]{1,2,0:T(8,128)S(1)}, u32[]{:S(2)}, u32[]{:S(2)}) async-start(f32[8,512,64]{1,2,0:T(8,128)} %broadcast_in_dim.10), calls=%async_computation.3 | async-start | bytes 2097152 | tf_op jit(solution)/shard_map/all_to_all | solution.py:20
  265.1 165.7 %copy-start.2 = (bf16[512,512]{0,1:T(8,128)(2,1)S(1)}, bf16[512,512]{0,1:T(8,128)(2,1)}, u32[]{:S(2)}) copy-start(bf16[512,512]{0,1:T(8,128)(2,1)} %all-reduce.5) | copy-start | bytes 1572868
  265.1 165.7 %copy-start.3 = (bf16[3584,64]{0,1:T(8,128)(2,1)S(1)}, bf16[3584,64]{0,1:T(8,128)(2,1)}, u32[]{:S(2)}) copy-start(bf16[3584,64]{0,1:T(8,128)(2,1)} %all-reduce.4) | copy-start | bytes 1376260
where the time goes:
time: 477 us; the launch traced here: 476 us
  blocking collectives  411 us (86%)
  matrix products  31.2 us (7%)
  starting transfers between devices  18 us (4%)
  local copies, waits for them, and re-layouts  5.72 us (1%)
  other arithmetic  4.84 us (1%)
    psum x1, blocking collectives, local(): rotated_grads = lax.psum(grad_part, DP_COL).astype(jnp.bfloat16)  166 us
    psum x1, blocking collectives, local(): rotated_inputs = lax.psum(input_part, ('dp', 'row')).astype(jnp.bfloat16)  91.8 us
    psum x1, blocking collectives, local(): lax.psum(sent_and_summed(left_part, 'dp', 1), COL).astype(jnp.bfloat16)  71.9 us
    psum x8, blocking collectives, by_axis(): shard = lax.psum(shard, axis)  71.1 us
    all_to_all x3, starting transfers between devices, copy_for_each(): return lax.all_to_all(copies, axis, split_axis=0, concat_axis=0, tiled=True)  14.3 us
    dot_general x2, matrix products, score_block(): jnp.dot(rotated_grads, precond, preferred_element_type=jnp.float32)  13.2 us
    all_to_all x1, blocking collectives, sent_and_summed(): tiles = lax.all_to_all(cut_along(shard, dim, count), axis, 0, 0, tiled=True)  10.3 us
    dot_general x1, matrix products, local(): jnp.dot(collect(out_grads, 'row', 0), basis_output, preferred_element_typ...  10.1 us
  transfers between devices with their start and end apart: 4, of which 1 were waited for; matrix products, arithmetic and copies ran while one was open for 5% of the time, Pallas kernels for 0%

commit v1 on v0

v1 whole, which is shorter than its diff:
```python
import jax
import jax.numpy as jnp
from jax import lax
from jax.experimental import pallas as pl
from jax.experimental.pallas import tpu as pltpu
from jax.sharding import PartitionSpec as P

DG = 28672
DA = 8192
RANK = 32
NQ = 4
TOK = 512
DAMP_RATIO = 0.1

NX = 4
NZ = 8
KB = 3584
KH = KB // 2
IB = 896
LB = 512
JB = 512
PW = 768
QW = KH - PW
TILE = 256

BF = jnp.bfloat16
F32 = jnp.float32
MESH = pl.DeviceIdType.MESH


def plane_scratch(tag, rows, kind):
    eighth, quarter = rows // 8, rows // 4
    V = pltpu.VMEM
    return {
        tag + "csp": V((2, rows, PW), kind),
        tag + "csq": V((2, rows, QW), kind),
        tag + "crp": V((2, rows, PW), kind),
        tag + "crq": V((2, rows, QW), kind),
        tag + "owp": V((2, rows, PW), F32),
        tag + "owq": V((2, rows, QW), F32),
        tag + "ps": V((2, rows, PW), kind),
        tag + "qs": V((2, 2, NX, eighth, QW), kind),
        tag + "pr": V((2, 3, quarter, PW), kind),
        tag + "qr": V((3, NX, eighth, QW), kind),
        tag + "p2": V((2, 2, eighth, PW), kind),
        tag + "p2f": V((2, 2, eighth, PW), F32),
        tag + "q2": V((NX, eighth, QW), kind),
        tag + "q2f": V((NX, eighth, QW), F32),
        tag + "pr2": V((3, eighth, PW), kind),
        tag + "qr2": V((3, eighth, QW), kind),
        tag + "f": V((2 * rows, KH), kind),
    }


def scratch():
    V = pltpu.VMEM
    shapes = {
        "x": V((TOK, IB), BF),
        "b": V((IB, KB), BF),
        "bin": V((JB, LB), BF),
        "eig": V((KH, LB), BF),
        "ql": V((IB, 128), BF),
        "qr": V((JB, 128), BF),
        "qlt": V((128, IB), BF),
        "y": V((8, 2, 32, JB), BF),
        "qrt": V((128, JB), BF),
        "ads": V((8, 96, 256), BF),
        "adr": V((8, 96, 256), BF),
        "ao": V((8, 80, 256), F32),
        "azs": V((8, 96, 256), BF),
        "azr": V((7, 96, 256), BF),
        "afin": V((2, 8, 80, 256), BF),
        "rm": V((NQ, 128, LB), BF),
        "lt": V((KH, 128), BF),
        "pq": V((NQ, KH, LB), BF),
        "m": V((TOK, 128), F32),
        "dmp": V((4, 8, 128), F32),
        "dmz": V((7, 8, 128), F32),
        "dmx": V((3, 8, 128), F32),
        "dmy": V((3, 8, 128), F32),
        "dmc": V((8, 128), F32),
        "fcs": V((2, 8, 128), F32),
        "fcr": V((8, 128), F32),
        "fzs": V((8, 128), F32),
        "fzr": V((7, 8, 128), F32),
        "fps": V((8, 128), F32),
        "fpr": V((15, 8, 128), F32),
        "fin": V((2, 8, 128), F32),
    }
    shapes.update(plane_scratch("l_", 64, F32))
    shapes.update(plane_scratch("g_", 256, BF))
    return shapes


N_SEM = 144
NAMES = tuple(scratch())


def kernel(xg, yg, b_hbm, bin_hbm, eig_hbm, ql_hbm, qr_hbm, out_ref, *refs):
    s = dict(zip(NAMES, refs))
    send_sems, recv_sems, local_sems = refs[len(NAMES) :]
    d = lax.axis_index("dp")
    r = lax.axis_index("row")
    c = lax.axis_index("col")
    x = c // 4
    yl = lax.rem(c // 2, 2)
    e = lax.rem(c, 2)

    def dev(dp=None, z=None, xx=None, yy=None, ee=None):
        dp = d if dp is None else dp
        z = r if z is None else z
        xx = x if xx is None else xx
        yy = yl if yy is None else yy
        ee = e if ee is None else ee
        return {"dp": dp, "row": z, "col": xx * 4 + yy * 2 + ee}

    def zp(off):
        return lax.rem(r + off, NZ)

    def xp(off):
        return lax.rem(x + off, NX)

    y_peers = ((1 - d, yl), (1 - d, 1 - yl), (d, 1 - yl))

    started = []
    local_started = []

    def send(src, dst, device):
        k = len(started)
        copy = pltpu.make_async_remote_copy(
            src_ref=src,
            dst_ref=dst,
            send_sem=send_sems.at[k],
            recv_sem=recv_sems.at[k],
            device_id=device,
            device_id_type=MESH,
        )
        copy.start()
        started.append(copy)
        return copy

    def fetch(src, dst):
        copy = pltpu.make_async_copy(src, dst, local_sems.at[len(local_started)])
        copy.start()
        local_started.append(copy)
        return copy

    def got(copies):
        for copy in copies:
            copy.wait_recv()

    def aligned(value, step):
        return pl.multiple_of(value, step)

    get_b = fetch(b_hbm, s["b"])
    get_ql = fetch(ql_hbm, s["ql"])
    get_qr = fetch(qr_hbm, s["qr"])
    get_bin = fetch(bin_hbm, s["bin"])
    get_eig = fetch(eig_hbm.at[pl.ds(aligned(d * KH, 256), KH)], s["eig"])

    def slot(z):
        return pl.ds(aligned(lax.rem(z + 4 * e, NZ) * 64, 64), 64)

    get_x = fetch(xg, s["x"].at[slot(r)])
    get_y = fetch(yg, s["y"].at[x * 2 + yl, e])

    barrier = pltpu.get_barrier_semaphore()
    peers = [dev(z=zp(off)) for off in range(1, NZ)]
    for off in range(NX):
        for dp, yy in ((d, yl),) + y_peers:
            if off or dp is not d or yy is not yl:
                peers.append(dev(dp=dp, xx=xp(off), yy=yy))
    peers.append(dev(ee=1 - e))
    for peer in peers:
        pl.semaphore_signal(barrier, inc=1, device_id=peer, device_id_type=MESH)
    pl.semaphore_wait(barrier, len(peers))

    right, left = dev(z=zp(1)), dev(z=zp(NZ - 1))

    def ring(block_right, block_left, part_right=None, part_left=None):
        def rows(z, part):
            base = lax.rem(z + 4 * e, NZ) * 64
            if part is None:
                return pl.ds(aligned(base, 64), 64)
            return pl.ds(aligned(base + part * 32, 32), 32)

        a = rows(block_right, part_right)
        b = rows(block_left, part_left)
        return [
            send(s["x"].at[a], s["x"].at[a], right),
            send(s["x"].at[b], s["x"].at[b], left),
        ]

    get_x.wait()
    z1 = ring(r, r)
    get_y.wait()
    mine = s["y"].at[x * 2 + yl, e]
    y_in = []
    for off in range(NX):
        for yy in (yl, 1 - yl):
            if off or yy is not yl:
                y_in.append(send(mine, mine, dev(xx=xp(off), yy=yy)))

    partner = dev(ee=1 - e)

    def partial_group(tag, rows, lhs, h, q_group):
        width = QW if q_group else PW
        own, out = (s[tag + "owq"], s[tag + "csq"]) if q_group else (s[tag + "owp"], s[tag + "csp"])
        landing = s[tag + "crq"] if q_group else s[tag + "crp"]
        base = h * KH + (PW if q_group else 0)

        def tile(j, carry):
            columns = pl.ds(aligned(base + j * TILE, 128), TILE)
            part = jnp.dot(lhs[...], s["b"][:, columns], preferred_element_type=F32)
            here = pl.ds(aligned(j * TILE, TILE), TILE)
            own[h, :, here] = part[:rows]
            out[h, :, here] = part[rows:].astype(out.dtype)
            return carry

        lax.fori_loop(0, width // TILE, tile, 0)
        return send(out.at[h], landing.at[h], partner)

    def chip_sum(tag, rows, h, q_group):
        eighth = rows // 8
        own = s[tag + "owq"] if q_group else s[tag + "owp"]
        landing = s[tag + "crq"] if q_group else s[tag + "crp"]
        out = s[tag + "qs"] if q_group else s[tag + "ps"]

        def chunk(i, carry):
            here = pl.ds(aligned(i * eighth, eighth), eighth)
            total = own[h, here, :] + landing[h, here, :].astype(F32)
            own[h, here, :] = total
            if q_group:
                out[h, lax.rem(i, 2), i // 2] = total.astype(out.dtype)
            else:
                out[h, here, :] = total.astype(out.dtype)
            return carry

        lax.fori_loop(0, 8, chunk, 0)

    def first_p(tag, rows, h, slot_h):
        quarter = rows // 4
        return [
            send(
                s[tag + "ps"].at[h, pl.ds(aligned(xp(off) * quarter, quarter), quarter)],
                s[tag + "pr"].at[h, off - 1],
                dev(xx=xp(off)),
            )
            for off in range(1, NX)
        ]

    def first_q(tag, which):
        return [
            send(s[tag + "qs"].at[dp, yy], s[tag + "qr"].at[i], dev(dp=dp, yy=yy))
            for i, (dp, yy) in enumerate(y_peers)
            if i in which
        ]

    def second_p(tag, rows, h, which):
        eighth, quarter = rows // 8, rows // 4
        for yy in range(2):
            here = pl.ds(aligned(x * quarter + yy * eighth, eighth), eighth)
            total = s[tag + "owp"][h, here, :]
            for i in range(3):
                total += s[tag + "pr"][h, i, yy * eighth : (yy + 1) * eighth, :].astype(F32)
            s[tag + "p2f"][h, yy] = total
            s[tag + "p2"][h, yy] = total.astype(s[tag + "p2"].dtype)
        return [
            send(s[tag + "p2"].at[dp, yy], s[tag + "pr2"].at[i], dev(dp=dp, yy=yy))
            for i, (dp, yy) in enumerate(y_peers)
            if i in which
        ]

    def second_q(tag, rows):
        eighth, quarter = rows // 8, rows // 4
        for xx in range(NX):
            here = pl.ds(aligned(xx * quarter + yl * eighth, eighth), eighth)
            total = s[tag + "owq"][d, here, :]
            for i in range(3):
                total += s[tag + "qr"][i, xx].astype(F32)
            s[tag + "q2f"][xx] = total
            s[tag + "q2"][xx] = total.astype(s[tag + "q2"].dtype)
        return [
            send(s[tag + "q2"].at[xp(off)], s[tag + "qr2"].at[off - 1], dev(xx=xp(off)))
            for off in range(1, NX)
        ]

    def last_sum(tag, rows):
        eighth, quarter = rows // 8, rows // 4
        here = pl.ds(aligned(e * rows + x * quarter + yl * eighth, eighth), eighth)
        kind = s[tag + "f"].dtype
        p_total = s[tag + "p2f"][d, yl]
        q_total = s[tag + "q2f"][x]
        for i in range(3):
            p_total += s[tag + "pr2"][i].astype(F32)
            q_total += s[tag + "qr2"][i].astype(F32)
        s[tag + "f"][here, :PW] = p_total.astype(kind)
        s[tag + "f"][here, PW:] = q_total.astype(kind)
        block = s[tag + "f"].at[here]
        copies = []
        for off in range(NX):
            for yy in (yl, 1 - yl):
                if off or yy is not yl:
                    copies.append(send(block, block, dev(xx=xp(off), yy=yy)))
        return copies

    def to_partner(tag, rows):
        block = s[tag + "f"].at[pl.ds(aligned(e * rows, rows), rows)]
        return [send(block, block, partner)]

    groups = ((1 - d, True), (1 - d, False), (d, True), (d, False))

    get_ql.wait()
    turned = s["ql"][...].astype(F32).T.astype(BF)
    s["qlt"][:64] = jnp.where(e == 0, turned[:64], turned[64:])
    s["qlt"][64:] = jnp.where(e == 0, turned[64:], turned[:64])
    get_qr.wait()
    s["qrt"][...] = s["qr"][...].astype(F32).T.astype(BF)
    get_b.wait()
    l_core = [partial_group("l_", 64, s["qlt"], h, q) for h, q in groups[:2]]
    got(z1)
    z2 = ring(zp(NZ - 1), zp(1))
    l_core += [partial_group("l_", 64, s["qlt"], h, q) for h, q in groups[2:]]

    get_eig.wait()

    def eig_sum(i, total):
        rows = s["eig"][pl.ds(aligned(i * 128, 128), 128), :].astype(F32)
        return total + jnp.sum(rows.reshape(16, 8, LB), axis=0)

    total = lax.fori_loop(0, KH // 128, eig_sum, jnp.zeros((8, LB), F32))
    s["dmp"][0] = total[:, :128] + total[:, 128:256] + total[:, 256:384] + total[:, 384:]
    dm_z = [send(s["dmp"].at[0], s["dmz"].at[off - 1], dev(z=zp(off))) for off in range(1, NZ)]

    def run_plane_first(tag, rows, core_copies):
        copies_q, copies_p = [], []
        for i, (h, q_group) in enumerate(groups):
            got([core_copies[i]])
            chip_sum(tag, rows, h, q_group)
            if q_group:
                copies_q += first_q(tag, (0, 1) if i == 0 else (2,))
            else:
                copies_p.append(first_p(tag, rows, h, i))
        return copies_q, copies_p

    l_q, l_p = run_plane_first("l_", 64, l_core)
    got(z2)
    z3 = ring(zp(NZ - 2), zp(2))

    got(y_in)
    y_half = s["y"].at[:, e]
    y_core = [send(y_half, y_half, partner)]

    got(dm_z)
    s["dmp"][1] = s["dmp"][0] + jnp.sum(s["dmz"][...], axis=0)
    dm_x = [send(s["dmp"].at[1], s["dmx"].at[off - 1], dev(xx=xp(off))) for off in range(1, NX)]

    got(l_q)
    l_q2 = second_q("l_", 64)
    got(l_p[0])
    l_p2 = second_p("l_", 64, 1 - d, (0, 1))
    got(l_p[1])
    l_p2 += second_p("l_", 64, d, (2,))

    got(z3)
    z4 = ring(zp(NZ - 3), zp(3), 0, 1)

    got(y_core)
    get_bin.wait()
    tokens = s["y"][...].reshape(TOK, JB)

    def input_parts(half):
        columns = pl.ds(aligned(half * 256, 256), 256)
        basis = s["bin"][:, columns]
        return (
            jnp.dot(tokens, basis, preferred_element_type=F32),
            jnp.dot(s["qrt"][...], basis, preferred_element_type=F32),
        )

    def put(dst, g, token_rows, factor_rows):
        dst[g, :64] = token_rows.astype(BF)
        high = factor_rows.astype(BF)
        dst[g, 64:80] = high
        dst[g, 80:] = (factor_rows - high.astype(F32)).astype(BF)

    token_part, factor_part = input_parts(1 - d)
    for g in range(8):
        put(s["ads"], g, token_part[g * 64 : (g + 1) * 64], factor_part[g * 16 : (g + 1) * 16])
    a_dp = [send(s["ads"], s["adr"], dev(dp=1 - d))]
    token_part, factor_part = input_parts(d)
    for g in range(8):
        s["ao"][g, :64] = token_part[g * 64 : (g + 1) * 64]
        s["ao"][g, 64:] = factor_part[g * 16 : (g + 1) * 16]

    got(dm_x)
    s["dmp"][2] = s["dmp"][1] + jnp.sum(s["dmx"][...], axis=0)
    dm_y = [
        send(s["dmp"].at[2], s["dmy"].at[i], dev(dp=dp, yy=yy)) for i, (dp, yy) in enumerate(y_peers)
    ]

    got(l_q2)
    got(l_p2)
    l_f = last_sum("l_", 64)

    got(z4)
    g_core = [partial_group("g_", 256, s["x"], *groups[0])]
    g_q, g_p = [], []
    for i, (h, q_group) in enumerate(groups):
        if i + 1 < len(groups):
            g_core.append(partial_group("g_", 256, s["x"], *groups[i + 1]))
        got([g_core[i]])
        chip_sum("g_", 256, h, q_group)
        if q_group:
            g_q += first_q("g_", (0, 1) if i == 0 else (2,))
        else:
            g_p.append(first_p("g_", 256, h, i))

    got(a_dp)

    def a_first(g, carry):
        landed = s["adr"]
        token_rows = s["ao"][g, :64] + landed[g, :64].astype(F32)
        factor_rows = s["ao"][g, 64:] + landed[g, 64:80].astype(F32) + landed[g, 80:].astype(F32)
        s["ao"][g, :64] = token_rows
        s["ao"][g, 64:] = factor_rows
        put(s["azs"], g, token_rows, factor_rows)
        return carry

    lax.fori_loop(0, 8, a_first, 0)
    a_z = [send(s["azs"].at[zp(off)], s["azr"].at[off - 1], dev(z=zp(off))) for off in range(1, NZ)]

    got(l_f)
    l_last = to_partner("l_", 64)
    got(dm_y)
    s["dmp"][3] = s["dmp"][2] + jnp.sum(s["dmy"][...], axis=0)
    dm_c = [send(s["dmp"].at[3], s["dmc"], partner)]

    got(a_z)
    token_rows = s["ao"][r, :64]
    factor_rows = s["ao"][r, 64:]
    for i in range(7):
        token_rows += s["azr"][i, :64].astype(F32)
        factor_rows += s["azr"][i, 64:80].astype(F32) + s["azr"][i, 80:].astype(F32)
    s["afin"][d, r, :64] = token_rows.astype(BF)
    s["afin"][d, r, 64:] = factor_rows.astype(BF)
    mine = s["afin"].at[d, r]
    a_f = [send(mine, mine, dev(z=zp(off))) for off in range(1, NZ)]

    got(g_q)
    g_q2 = second_q("g_", 256)
    got(g_p[0])
    g_p2 = second_p("g_", 256, 1 - d, (0, 1))
    got(g_p[1])
    g_p2 += second_p("g_", 256, d, (2,))

    got(a_f)
    mine = s["afin"].at[d]
    a_last = [send(mine, mine, dev(dp=1 - d))]

    got(g_q2)
    got(g_p2)
    g_f = last_sum("g_", 256)

    got(dm_c)
    damping = jnp.sum(s["dmp"][3] + s["dmc"][...], keepdims=True) * (DAMP_RATIO / (DG * DA))
    got(l_last)
    s["lt"][...] = s["l_f"][...].T.astype(BF)
    got(a_last)
    for q in range(NQ):
        s["rm"][q] = jnp.zeros((128, LB), BF)
        for g in range(2):
            rows = slice(q * RANK + g * 16, q * RANK + (g + 1) * 16)
            for half in range(2):
                s["rm"][q, rows, half * 256 : (half + 1) * 256] = s["afin"][half, q * 2 + g, 64:]

    def precondition(i, carry):
        rows = pl.ds(aligned(i * 128, 128), 128)
        inverse = 1.0 / (s["eig"][rows, :].astype(F32) + damping)
        left_rows = s["lt"][rows, :]
        for q in range(NQ):
            product = jnp.dot(left_rows, s["rm"][q], preferred_element_type=F32)
            s["pq"][q, rows, :] = (product * inverse).astype(BF)
        return carry

    lax.fori_loop(0, KH // 128, precondition, 0)

    got(g_f)
    g_last = to_partner("g_", 256)
    lanes = lax.broadcasted_iota(jnp.int32, (TILE, 128), 1)
    token_group = lax.broadcasted_iota(jnp.int32, (TILE, 128), 0) // 128

    def score(half):
        here = pl.ds(aligned(half * 256, 256), 256)
        s["m"][here, :] = jnp.zeros((TILE, 128), F32)

        def one_query(q, carry):
            weighted = jnp.dot(s["g_f"][here, :], s["pq"][q], preferred_element_type=F32)
            total = jnp.zeros((TILE, 128), F32)
            for part in range(2):
                inputs = s["afin"][part, pl.ds(half * 4, 4), :64, :].astype(F32).reshape(TILE, 256)
                terms = weighted[:, part * 256 : (part + 1) * 256] * inputs
                total += terms[:, :128] + terms[:, 128:]
            scores = jnp.sum(total, axis=1, keepdims=True)
            s["m"][here, :] += jnp.where(lanes == q + 4 * token_group, scores, 0.0)
            return carry

        lax.fori_loop(0, NQ, one_query, 0)

    score(e)
    got(g_last)
    score(1 - e)

    turned = s["m"][...].T[:8]
    for half in range(2):
        base = half * 256
        s["fcs"][half] = turned[:, base : base + 128] + turned[:, base + 128 : base + 256]
    f_core = [send(s["fcs"].at[1 - e], s["fcr"], partner)]
    got(f_core)
    s["fzs"][...] = s["fcs"][e] + s["fcr"][...]
    f_z = [send(s["fzs"], s["fzr"].at[off - 1], dev(z=zp(off))) for off in range(1, NZ)]
    got(f_z)
    s["fps"][...] = s["fzs"][...] + jnp.sum(s["fzr"][...], axis=0)
    f_plane = []
    for off in range(NX):
        for dp, yy in ((d, yl),) + y_peers:
            if off or dp is not d or yy is not yl:
                f_plane.append(send(s["fps"], s["fpr"].at[len(f_plane)], dev(dp=dp, xx=xp(off), yy=yy)))
    got(f_plane)
    s["fin"][e] = s["fps"][...] + jnp.sum(s["fpr"][...], axis=0)
    mine = s["fin"].at[e]
    f_last = [send(mine, mine, partner)]
    got(f_last)
    for half in range(2):
        for part in range(2):
            columns = slice((half * 2 + part) * 128, (half * 2 + part + 1) * 128)
            low = s["fin"][half, part * 4 : part * 4 + 2, :]
            high = s["fin"][half, part * 4 + 2 : part * 4 + 4, :]
            out_ref[:, columns] = jnp.where(d == 0, low, high)

    for copy in started:
        copy.wait_send()


def local(out_grads, layer_inputs, basis_output, basis_input, eigenvalues, query_left, query_right):
    any_space = pl.BlockSpec(memory_space=pl.ANY)
    return pl.pallas_call(
        kernel,
        out_shape=jax.ShapeDtypeStruct((2, TOK), F32),
        in_specs=[any_space] * 7,
        out_specs=pl.BlockSpec(memory_space=pltpu.VMEM),
        scratch_shapes=list(scratch().values())
        + [
            pltpu.SemaphoreType.DMA((N_SEM,)),
            pltpu.SemaphoreType.DMA((N_SEM,)),
            pltpu.SemaphoreType.DMA((8,)),
        ],
        compiler_params=pltpu.CompilerParams(
            collective_id=0, has_side_effects=True, vmem_limit_bytes=60 * 1024 * 1024
        ),
        cost_estimate=pl.CostEstimate(flops=9_000_000_000, bytes_accessed=11_000_000, transcendentals=0),
    )(out_grads, layer_inputs, basis_output, basis_input, eigenvalues, query_left, query_right)


def solution(mesh):
    in_specs = (
        P("row", ("dp", "col")),
        P("col", ("dp", "row")),
        P(("dp", "col"), "row"),
        P(("dp", "row"), "col"),
        P("row", "col"),
        P(("dp", "col"), None),
        P(("dp", "row"), None),
    )
    return jax.shard_map(
        local, mesh=mesh, in_specs=in_specs, out_specs=P("dp", None), check_vma=False
    )
```

time: 477 us -> 103 us (0.22)
  blocking collectives: 411 us -> 0 us
  Pallas kernels: 0 us -> 101 us
  matrix products: 31.2 us -> 0 us
  starting transfers between devices: 18 us -> 0 us
  other arithmetic: 4.84 us -> 0 us
    psum x11 -> x0, blocking collectives: 400 us -> none  [the longest x1 166 us: local(): rotated_grads = lax.psum(grad_part, DP_COL).astype(jnp.bfloat16)]
    pallas_call x0 -> x1, Pallas kernels: none -> 101 us  [local(): pl.pallas_call(kernel, out_shape=jax.ShapeDtypeStruct((2, TOK), F32), in_...]
    dot_general x6 -> x0, matrix products: 31.2 us -> none  [the longest x2 13.2 us: score_block(): jnp.dot(rotated_grads, precond, preferred_element_type=jnp.float32)]
    all_to_all x4 -> x0, starting transfers between devices: 18 us -> none  [the longest x3 14.3 us: copy_for_each(): return lax.all_to_all(copies, axis, split_axis=0, concat_axis=0, tiled=True)]
    all_to_all x1 -> x0, blocking collectives: 10.3 us -> none  [sent_and_summed(): tiles = lax.all_to_all(cut_along(shard, dim, count), axis, 0, 0, tiled=True)]
    reduce_sum x4 -> x0, other arithmetic: 4.83 us -> none  [the longest x1 4.53 us: local(): eigen_total = by_axis(jnp.sum(eigenvalues.astype(jnp.float32)), ROW_COL)]
  transfers between devices with their start and end apart: 4 -> 0, of which waited for: 1 -> 0; matrix products, arithmetic and copies ran while one was open for 5% -> 0% of each run, Pallas kernels for 0% -> 0%
where the time goes in v1:
time: 103 us
  Pallas kernels  101 us (98%)
  local copies, waits for them, and re-layouts  1.28 us (1%)
    pallas_call x1, Pallas kernels, local(): pl.pallas_call(kernel, out_shape=jax.ShapeDtypeStruct((2, TOK), F32), in_...  101 us

profile of v1, /device:TPU:1, one launch (start us, length us, event | category | flops | bytes accessed | tf_op | source)
XLA Modules:
  0.0 102.6 jit_solution(13520086450788264597)
XLA Ops:
  0.0 101.3 %shard_map.73 = f32[2,512]{1,0:T(2,128)} custom-call(bf16[64,896]{1,0:T(8,128)(2,1)} %xg.1, bf16[32,512]{1,0:T(8,128)(2,1)} %yg.1, bf16[896,3584]{1,0:T(8,128)(2,1)} %b_hbm.1, bf16[512,512]{1,0:T(8,128)(2,1)} %bin_hbm.1, bf16[3584,512]{1,0:T(8,128)(2,1)} %eig_hbm.1, bf16[896,128]{1,0:T(8,128)(2,1)} %ql_hbm.1, bf16[512,128]{1,0:T(8,128)(2,1)} %qr_hbm.1), custom_call_target="tpu_custom_call" | custom-call | flops 8999999488 | bytes 11000000 | tf_op jit(solution)/shard_map/pallas_call | solution.py:546
  101.3 1.3 %copy.9 = f32[2,512]{1,0:T(2,128)} copy(f32[2,512]{1,0:T(2,128)} %shard_map.73) | data formatting | bytes 8192

commit v2 on v1

--- a/solution.py
+++ b/solution.py
@@ -22,6 +22,8 @@
 PW = 768
 QW = KH - PW
 TILE = 256
+ROWS = 128
+ORDER = (0, -1, 1, -2, 2, -3, 3, 4)
 
 BF = jnp.bfloat16
 F32 = jnp.float32
@@ -48,14 +50,14 @@
         tag + "q2f": V((NX, eighth, QW), F32),
         tag + "pr2": V((3, eighth, PW), kind),
         tag + "qr2": V((3, eighth, QW), kind),
-        tag + "f": V((2 * rows, KH), kind),
+        tag + "f": V((2 * rows, KH), BF) if rows >= 128 else V((16, 16, KH // 2), BF),
     }
 
 
 def scratch():
     V = pltpu.VMEM
     shapes = {
-        "x": V((TOK, IB), BF),
+        "x": V((2, 2 * ROWS, IB), BF),
         "b": V((IB, KB), BF),
         "bin": V((JB, LB), BF),
         "eig": V((KH, LB), BF),
@@ -64,15 +66,22 @@
         "qlt": V((128, IB), BF),
         "y": V((8, 2, 32, JB), BF),
         "qrt": V((128, JB), BF),
-        "ads": V((8, 96, 256), BF),
-        "adr": V((8, 96, 256), BF),
-        "ao": V((8, 80, 256), F32),
-        "azs": V((8, 96, 256), BF),
-        "azr": V((7, 96, 256), BF),
-        "afin": V((2, 8, 80, 256), BF),
+        "rs": V((8, 16, 256), F32),
+        "rr": V((8, 16, 256), F32),
+        "ro": V((8, 16, 256), F32),
+        "rzr": V((7, 16, 256), F32),
+        "rfin": V((2, 8, 16, 256), BF),
+        "ads": V((8, 64, 256), BF),
+        "adr": V((8, 64, 256), BF),
+        "ao": V((8, 64, 256), F32),
+        "azs": V((8, 64, 256), BF),
+        "azr": V((7, 64, 256), BF),
+        "afin": V((2, 8, 64, 256), BF),
         "rm": V((NQ, 128, LB), BF),
         "lt": V((KH, 128), BF),
         "pq": V((NQ, KH, LB), BF),
+        "at": V((2 * ROWS, LB), F32),
+        "mc": V((2 * ROWS, 128), F32),
         "m": V((TOK, 128), F32),
         "dmp": V((4, 8, 128), F32),
         "dmz": V((7, 8, 128), F32),
@@ -88,11 +97,12 @@
         "fin": V((2, 8, 128), F32),
     }
     shapes.update(plane_scratch("l_", 64, F32))
-    shapes.update(plane_scratch("g_", 256, BF))
+    shapes.update(plane_scratch("a_", ROWS, BF))
+    shapes.update(plane_scratch("b_", ROWS, BF))
     return shapes
 
 
-N_SEM = 144
+N_SEM = 176
 NAMES = tuple(scratch())
 
 
@@ -158,10 +168,14 @@
     get_bin = fetch(bin_hbm, s["bin"])
     get_eig = fetch(eig_hbm.at[pl.ds(aligned(d * KH, 256), KH)], s["eig"])
 
-    def slot(z):
-        return pl.ds(aligned(lax.rem(z + 4 * e, NZ) * 64, 64), 64)
-
-    get_x = fetch(xg, s["x"].at[slot(r)])
+    def place(rel, part=None):
+        position = ORDER.index(rel)
+        base = lax.rem(position % 4 + 2 * e, 4) * 64
+        if part is None:
+            return s["x"].at[position // 4, pl.ds(aligned(base, 64), 64)]
+        return s["x"].at[position // 4, pl.ds(aligned(base + part * 32, 32), 32)]
+
+    get_x = fetch(xg, place(0))
     get_y = fetch(yg, s["y"].at[x * 2 + yl, e])
 
     barrier = pltpu.get_barrier_semaphore()
@@ -173,33 +187,21 @@
     peers.append(dev(ee=1 - e))
     for peer in peers:
         pl.semaphore_signal(barrier, inc=1, device_id=peer, device_id_type=MESH)
-    pl.semaphore_wait(barrier, len(peers))
-
     right, left = dev(z=zp(1)), dev(z=zp(NZ - 1))
 
-    def ring(block_right, block_left, part_right=None, part_left=None):
-        def rows(z, part):
-            base = lax.rem(z + 4 * e, NZ) * 64
-            if part is None:
-                return pl.ds(aligned(base, 64), 64)
-            return pl.ds(aligned(base + part * 32, 32), 32)
-
-        a = rows(block_right, part_right)
-        b = rows(block_left, part_left)
-        return [
-            send(s["x"].at[a], s["x"].at[a], right),
-            send(s["x"].at[b], s["x"].at[b], left),
-        ]
-
-    get_x.wait()
-    z1 = ring(r, r)
-    get_y.wait()
-    mine = s["y"].at[x * 2 + yl, e]
-    y_in = []
-    for off in range(NX):
-        for yy in (yl, 1 - yl):
-            if off or yy is not yl:
-                y_in.append(send(mine, mine, dev(xx=xp(off), yy=yy)))
+    def along_z(distance, parts_right=(0, 1), parts_left=(0, 1)):
+        copies = []
+        for part in range(2):
+            if distance:
+                got(z_in[part])
+            if part in parts_right:
+                far = 4 if distance == 3 else -distance - 1
+                copies.append([send(place(-distance, part), place(far, part), right)])
+            else:
+                copies.append([])
+            if part in parts_left:
+                copies[-1].append(send(place(distance, part), place(distance + 1, part), left))
+        return copies
 
     partner = dev(ee=1 - e)
 
@@ -218,7 +220,7 @@
             return carry
 
         lax.fori_loop(0, width // TILE, tile, 0)
-        return send(out.at[h], landing.at[h], partner)
+        return lambda: send(out.at[h], landing.at[h], partner)
 
     def chip_sum(tag, rows, h, q_group):
         eighth = rows // 8
@@ -288,15 +290,20 @@
     def last_sum(tag, rows):
         eighth, quarter = rows // 8, rows // 4
         here = pl.ds(aligned(e * rows + x * quarter + yl * eighth, eighth), eighth)
-        kind = s[tag + "f"].dtype
         p_total = s[tag + "p2f"][d, yl]
         q_total = s[tag + "q2f"][x]
         for i in range(3):
             p_total += s[tag + "pr2"][i].astype(F32)
             q_total += s[tag + "qr2"][i].astype(F32)
-        s[tag + "f"][here, :PW] = p_total.astype(kind)
-        s[tag + "f"][here, PW:] = q_total.astype(kind)
-        block = s[tag + "f"].at[here]
+        if rows >= 128:
+            s[tag + "f"][here, :PW] = p_total.astype(BF)
+            s[tag + "f"][here, PW:] = q_total.astype(BF)
+            block = s[tag + "f"].at[here]
+        else:
+            whole = jnp.concatenate([p_total, q_total], axis=1)
+            halves = [whole[:, : KH // 2], whole[:, KH // 2 :]]
+            s[tag + "f"][e * 8 + x * 2 + yl] = jnp.concatenate(halves, axis=0).astype(BF)
+            block = s[tag + "f"].at[e * 8 + x * 2 + yl]
         copies = []
         for off in range(NX):
             for yy in (yl, 1 - yl):
@@ -305,7 +312,8 @@
         return copies
 
     def to_partner(tag, rows):
-        block = s[tag + "f"].at[pl.ds(aligned(e * rows, rows), rows)]
+        count = rows if rows >= 128 else 8
+        block = s[tag + "f"].at[pl.ds(aligned(e * count, count), count)]
         return [send(block, block, partner)]
 
     groups = ((1 - d, True), (1 - d, False), (d, True), (d, False))
@@ -316,11 +324,46 @@
     s["qlt"][64:] = jnp.where(e == 0, turned[64:], turned[:64])
     get_qr.wait()
     s["qrt"][...] = s["qr"][...].astype(F32).T.astype(BF)
+    get_x.wait()
+    get_y.wait()
     get_b.wait()
-    l_core = [partial_group("l_", 64, s["qlt"], h, q) for h, q in groups[:2]]
-    got(z1)
-    z2 = ring(zp(NZ - 1), zp(1))
-    l_core += [partial_group("l_", 64, s["qlt"], h, q) for h, q in groups[2:]]
+    l_ready = [partial_group("l_", 64, s["qlt"], h, q) for h, q in groups[:2]]
+    pl.semaphore_wait(barrier, len(peers))
+
+    z_in = along_z(0)
+    mine = s["y"].at[x * 2 + yl, e]
+    y_in = []
+    for off in range(NX):
+        for yy in (yl, 1 - yl):
+            if off or yy is not yl:
+                y_in.append(send(mine, mine, dev(xx=xp(off), yy=yy)))
+    l_core = [start() for start in l_ready]
+
+    def half_columns(half):
+        return pl.ds(aligned(half * 256, 256), 256)
+
+    get_bin.wait()
+    factor_part = jnp.dot(s["qrt"][...], s["bin"][:, half_columns(1 - d)], preferred_element_type=F32)
+    s["rs"][...] = factor_part.reshape(8, 16, 256)
+    r_dp = [send(s["rs"], s["rr"], dev(dp=1 - d))]
+    factor_part = jnp.dot(s["qrt"][...], s["bin"][:, half_columns(d)], preferred_element_type=F32)
+    s["ro"][...] = factor_part.reshape(8, 16, 256)
+
+    l_core += [partial_group("l_", 64, s["qlt"], h, q)() for h, q in groups[2:]]
+
+    def first_steps(tag, rows, core_copies, i):
+        h, q_group = groups[i]
+        got([core_copies[i]])
+        chip_sum(tag, rows, h, q_group)
+        if q_group:
+            return first_q(tag, (0, 1) if i == 0 else (2,))
+        return first_p(tag, rows, h, i)
+
+    l_first = [first_steps("l_", 64, l_core, i) for i in range(4)]
+    z_in = along_z(1)
+    got(y_in)
+    y_half = s["y"].at[:, e]
+    y_core = [send(y_half, y_half, partner)]
 
     get_eig.wait()
 
@@ -332,65 +375,68 @@
     s["dmp"][0] = total[:, :128] + total[:, 128:256] + total[:, 256:384] + total[:, 384:]
     dm_z = [send(s["dmp"].at[0], s["dmz"].at[off - 1], dev(z=zp(off))) for off in range(1, NZ)]
 
-    def run_plane_first(tag, rows, core_copies):
-        copies_q, copies_p = [], []
-        for i, (h, q_group) in enumerate(groups):
-            got([core_copies[i]])
-            chip_sum(tag, rows, h, q_group)
-            if q_group:
-                copies_q += first_q(tag, (0, 1) if i == 0 else (2,))
-            else:
-                copies_p.append(first_p(tag, rows, h, i))
-        return copies_q, copies_p
-
-    l_q, l_p = run_plane_first("l_", 64, l_core)
-    got(z2)
-    z3 = ring(zp(NZ - 2), zp(2))
-
-    got(y_in)
-    y_half = s["y"].at[:, e]
-    y_core = [send(y_half, y_half, partner)]
+    got(r_dp)
+    s["ro"][...] += s["rr"][...]
+    r_z = [send(s["ro"].at[zp(off)], s["rzr"].at[off - 1], dev(z=zp(off))) for off in range(1, NZ)]
+
+    got(y_core)
+    token_part = jnp.dot(
+        s["y"][...].reshape(TOK, JB), s["bin"][:, half_columns(1 - d)], preferred_element_type=F32
+    )
+    s["ads"][...] = token_part.reshape(8, 64, 256).astype(BF)
+    a_dp = [send(s["ads"], s["adr"], dev(dp=1 - d))]
+    token_part = jnp.dot(
+        s["y"][...].reshape(TOK, JB), s["bin"][:, half_columns(d)], preferred_element_type=F32
+    )
+    s["ao"][...] = token_part.reshape(8, 64, 256)
+
+    z_in = along_z(2)
+
+    a_core, a_first_in = [], []
+    for i in range(2):
+        a_core.append(partial_group("a_", ROWS, s["x"].at[0], *groups[i])())
+    a_first_in.append(first_steps("a_", ROWS, a_core, 0))
+    z_in = along_z(3, (0,), (1,))
+    for i in range(2, 4):
+        a_core.append(partial_group("a_", ROWS, s["x"].at[0], *groups[i])())
+        a_first_in.append(first_steps("a_", ROWS, a_core, i - 1))
+    a_first_in.append(first_steps("a_", ROWS, a_core, 3))
+
+    got(a_dp)
+    summed = s["ao"][...] + s["adr"][...].astype(F32)
+    s["ao"][...] = summed
+    s["azs"][...] = summed.astype(BF)
+    a_z = [send(s["azs"].at[zp(off)], s["azr"].at[off - 1], dev(z=zp(off))) for off in range(1, NZ)]
 
     got(dm_z)
     s["dmp"][1] = s["dmp"][0] + jnp.sum(s["dmz"][...], axis=0)
     dm_x = [send(s["dmp"].at[1], s["dmx"].at[off - 1], dev(xx=xp(off))) for off in range(1, NX)]
 
-    got(l_q)
-    l_q2 = second_q("l_", 64)
-    got(l_p[0])
-    l_p2 = second_p("l_", 64, 1 - d, (0, 1))
-    got(l_p[1])
-    l_p2 += second_p("l_", 64, d, (2,))
-
-    got(z3)
-    z4 = ring(zp(NZ - 3), zp(3), 0, 1)
-
-    got(y_core)
-    get_bin.wait()
-    tokens = s["y"][...].reshape(TOK, JB)
-
-    def input_parts(half):
-        columns = pl.ds(aligned(half * 256, 256), 256)
-        basis = s["bin"][:, columns]
-        return (
-            jnp.dot(tokens, basis, preferred_element_type=F32),
-            jnp.dot(s["qrt"][...], basis, preferred_element_type=F32),
-        )
-
-    def put(dst, g, token_rows, factor_rows):
-        dst[g, :64] = token_rows.astype(BF)
-        high = factor_rows.astype(BF)
-        dst[g, 64:80] = high
-        dst[g, 80:] = (factor_rows - high.astype(F32)).astype(BF)
-
-    token_part, factor_part = input_parts(1 - d)
-    for g in range(8):
-        put(s["ads"], g, token_part[g * 64 : (g + 1) * 64], factor_part[g * 16 : (g + 1) * 16])
-    a_dp = [send(s["ads"], s["adr"], dev(dp=1 - d))]
-    token_part, factor_part = input_parts(d)
-    for g in range(8):
-        s["ao"][g, :64] = token_part[g * 64 : (g + 1) * 64]
-        s["ao"][g, 64:] = factor_part[g * 16 : (g + 1) * 16]
+    def second_steps(tag, rows, first):
+        got(first[0])
+        got(first[2])
+        copies = second_q(tag, rows)
+        got(first[1])
+        copies += second_p(tag, rows, 1 - d, (0, 1))
+        got(first[3])
+        return copies + second_p(tag, rows, d, (2,))
+
+    l_second = second_steps("l_", 64, l_first)
+
+    got(z_in[0])
+    got(z_in[1])
+    b_core, b_first_in = [], []
+    for i in range(4):
+        b_core.append(partial_group("b_", ROWS, s["x"].at[1], *groups[i])())
+        if i:
+            b_first_in.append(first_steps("b_", ROWS, b_core, i - 1))
+    b_first_in.append(first_steps("b_", ROWS, b_core, 3))
+
+    got(r_z)
+    factors = s["ro"][r] + jnp.sum(s["rzr"][...], axis=0)
+    s["rfin"][d, r] = factors.astype(BF)
+    mine = s["rfin"].at[d, r]
+    r_f = [send(mine, mine, dev(z=zp(off))) for off in range(1, NZ)]
 
     got(dm_x)
     s["dmp"][2] = s["dmp"][1] + jnp.sum(s["dmx"][...], axis=0)
@@ -398,80 +444,46 @@
         send(s["dmp"].at[2], s["dmy"].at[i], dev(dp=dp, yy=yy)) for i, (dp, yy) in enumerate(y_peers)
     ]
 
-    got(l_q2)
-    got(l_p2)
+    got(l_second)
     l_f = last_sum("l_", 64)
 
-    got(z4)
-    g_core = [partial_group("g_", 256, s["x"], *groups[0])]
-    g_q, g_p = [], []
-    for i, (h, q_group) in enumerate(groups):
-        if i + 1 < len(groups):
-            g_core.append(partial_group("g_", 256, s["x"], *groups[i + 1]))
-        got([g_core[i]])
-        chip_sum("g_", 256, h, q_group)
-        if q_group:
-            g_q += first_q("g_", (0, 1) if i == 0 else (2,))
-        else:
-            g_p.append(first_p("g_", 256, h, i))
-
-    got(a_dp)
-
-    def a_first(g, carry):
-        landed = s["adr"]
-        token_rows = s["ao"][g, :64] + landed[g, :64].astype(F32)
-        factor_rows = s["ao"][g, 64:] + landed[g, 64:80].astype(F32) + landed[g, 80:].astype(F32)
-        s["ao"][g, :64] = token_rows
-        s["ao"][g, 64:] = factor_rows
-        put(s["azs"], g, token_rows, factor_rows)
-        return carry
-
-    lax.fori_loop(0, 8, a_first, 0)
-    a_z = [send(s["azs"].at[zp(off)], s["azr"].at[off - 1], dev(z=zp(off))) for off in range(1, NZ)]
-
-    got(l_f)
-    l_last = to_partner("l_", 64)
+    a_second = second_steps("a_", ROWS, a_first_in)
+
+    got(a_z)
+    summed = s["ao"][r]
+    for i in range(7):
+        summed += s["azr"][i].astype(F32)
+    s["afin"][d, r] = summed.astype(BF)
+    mine = s["afin"].at[d, r]
+    a_f = [send(mine, mine, dev(z=zp(off))) for off in range(1, NZ)]
+
+    got(r_f)
+    mine = s["rfin"].at[d]
+    r_last = [send(mine, mine, dev(dp=1 - d))]
     got(dm_y)
     s["dmp"][3] = s["dmp"][2] + jnp.sum(s["dmy"][...], axis=0)
     dm_c = [send(s["dmp"].at[3], s["dmc"], partner)]
-
-    got(a_z)
-    token_rows = s["ao"][r, :64]
-    factor_rows = s["ao"][r, 64:]
-    for i in range(7):
-        token_rows += s["azr"][i, :64].astype(F32)
-        factor_rows += s["azr"][i, 64:80].astype(F32) + s["azr"][i, 80:].astype(F32)
-    s["afin"][d, r, :64] = token_rows.astype(BF)
-    s["afin"][d, r, 64:] = factor_rows.astype(BF)
-    mine = s["afin"].at[d, r]
-    a_f = [send(mine, mine, dev(z=zp(off))) for off in range(1, NZ)]
-
-    got(g_q)
-    g_q2 = second_q("g_", 256)
-    got(g_p[0])
-    g_p2 = second_p("g_", 256, 1 - d, (0, 1))
-    got(g_p[1])
-    g_p2 += second_p("g_", 256, d, (2,))
-
-    got(a_f)
-    mine = s["afin"].at[d]
-    a_last = [send(mine, mine, dev(dp=1 - d))]
-
-    got(g_q2)
-    got(g_p2)
-    g_f = last_sum("g_", 256)
+    got(l_f)
+    l_last = to_partner("l_", 64)
+
+    got(a_second)
+    a_out = last_sum("a_", ROWS)
+
+    b_second = second_steps("b_", ROWS, b_first_in)
 
     got(dm_c)
     damping = jnp.sum(s["dmp"][3] + s["dmc"][...], keepdims=True) * (DAMP_RATIO / (DG * DA))
     got(l_last)
-    s["lt"][...] = s["l_f"][...].T.astype(BF)
-    got(a_last)
+    for i in range(2):
+        left_rows = s["l_f"][...].astype(F32)[:, i * 8 : (i + 1) * 8].reshape(128, KH // 2)
+        s["lt"][i * (KH // 2) : (i + 1) * (KH // 2)] = left_rows.T.astype(BF)
+    got(r_last)
     for q in range(NQ):
         s["rm"][q] = jnp.zeros((128, LB), BF)
         for g in range(2):
             rows = slice(q * RANK + g * 16, q * RANK + (g + 1) * 16)
             for half in range(2):
-                s["rm"][q, rows, half * 256 : (half + 1) * 256] = s["afin"][half, q * 2 + g, 64:]
+                s["rm"][q, rows, half * 256 : (half + 1) * 256] = s["rfin"][half, q * 2 + g]
 
     def precondition(i, carry):
         rows = pl.ds(aligned(i * 128, 128), 128)
@@ -484,31 +496,51 @@
 
     lax.fori_loop(0, KH // 128, precondition, 0)
 
-    got(g_f)
-    g_last = to_partner("g_", 256)
-    lanes = lax.broadcasted_iota(jnp.int32, (TILE, 128), 1)
-    token_group = lax.broadcasted_iota(jnp.int32, (TILE, 128), 0) // 128
-
-    def score(half):
-        here = pl.ds(aligned(half * 256, 256), 256)
-        s["m"][here, :] = jnp.zeros((TILE, 128), F32)
+    got(a_f)
+    mine = s["afin"].at[d]
+    a_last = [send(mine, mine, dev(dp=1 - d))]
+
+    got(b_second)
+    b_out = last_sum("b_", ROWS)
+
+    got(a_out)
+    a_both = to_partner("a_", ROWS)
+    got(a_last)
+
+    lanes = lax.broadcasted_iota(jnp.int32, (2 * ROWS, 128), 1)
+    block_of = lax.broadcasted_iota(jnp.int32, (2 * ROWS, 128), 0) // 64
+
+    def score(tag, chunk):
+        blocks = [lax.rem(r + ORDER[chunk * 4 + j] + NZ, NZ) for j in range(4)]
+        odd = jnp.zeros_like(lanes)
+        for j, block in enumerate(blocks):
+            odd = jnp.where(block_of == j, lax.rem(block // 2, 2), odd)
+            for half in range(2):
+                columns = slice(half * 256, (half + 1) * 256)
+                s["at"][j * 64 : (j + 1) * 64, columns] = s["afin"][half, block].astype(F32)
+        s["mc"][...] = jnp.zeros((2 * ROWS, 128), F32)
 
         def one_query(q, carry):
-            weighted = jnp.dot(s["g_f"][here, :], s["pq"][q], preferred_element_type=F32)
-            total = jnp.zeros((TILE, 128), F32)
-            for part in range(2):
-                inputs = s["afin"][part, pl.ds(half * 4, 4), :64, :].astype(F32).reshape(TILE, 256)
-                terms = weighted[:, part * 256 : (part + 1) * 256] * inputs
-                total += terms[:, :128] + terms[:, 128:]
+            weighted = jnp.dot(s[tag + "f"][...], s["pq"][q], preferred_element_type=F32)
+            terms = weighted * s["at"][...]
+            total = terms[:, :128] + terms[:, 128:256] + terms[:, 256:384] + terms[:, 384:]
             scores = jnp.sum(total, axis=1, keepdims=True)
-            s["m"][here, :] += jnp.where(lanes == q + 4 * token_group, scores, 0.0)
+            s["mc"][...] += jnp.where(lanes == q + 4 * odd, scores, 0.0)
             return carry
 
         lax.fori_loop(0, NQ, one_query, 0)
-
-    score(e)
-    got(g_last)
-    score(1 - e)
+        for j, block in enumerate(blocks):
+            s["m"][pl.ds(aligned(block * 64, 64), 64), :] = s["mc"][j * 64 : (j + 1) * 64, :]
+
+    got(a_both)
+    score("a_", 0)
+    drained = len(started)
+    for copy in started[: drained - 8]:
+        copy.wait_send()
+    got(b_out)
+    b_both = to_partner("b_", ROWS)
+    got(b_both)
+    score("b_", 1)
 
     turned = s["m"][...].T[:8]
     for half in range(2):
@@ -537,7 +569,7 @@
             high = s["fin"][half, part * 4 + 2 : part * 4 + 4, :]
             out_ref[:, columns] = jnp.where(d == 0, low, high)
 
-    for copy in started:
+    for copy in started[drained - 8 :]:
         copy.wait_send()
 
 

time: 103 us -> 91.6 us (0.89)
  Pallas kernels: 101 us -> 90.2 us
    pallas_call x1, Pallas kernels: 101 us -> 90.2 us  [local(): pl.pallas_call(kernel, out_shape=jax.ShapeDtypeStruct((2, TOK), F32), in_...]
where the time goes in v2:
time: 91.6 us; the launch traced here: 91.5 us
  Pallas kernels  90.2 us (98%)
  local copies, waits for them, and re-layouts  1.28 us (1%)
    pallas_call x1, Pallas kernels, local(): pl.pallas_call(kernel, out_shape=jax.ShapeDtypeStruct((2, TOK), F32), in_...  90.2 us

profile of v2, /device:TPU:1, one launch (start us, length us, event | category | flops | bytes accessed | tf_op | source)
XLA Modules:
  0.0 91.5 jit_solution(9627737558745677643)
XLA Ops:
  0.0 90.2 %shard_map.73 = f32[2,512]{1,0:T(2,128)} custom-call(bf16[64,896]{1,0:T(8,128)(2,1)} %xg.1, bf16[32,512]{1,0:T(8,128)(2,1)} %yg.1, bf16[896,3584]{1,0:T(8,128)(2,1)} %b_hbm.1, bf16[512,512]{1,0:T(8,128)(2,1)} %bin_hbm.1, bf16[3584,512]{1,0:T(8,128)(2,1)} %eig_hbm.1, bf16[896,128]{1,0:T(8,128)(2,1)} %ql_hbm.1, bf16[512,128]{1,0:T(8,128)(2,1)} %qr_hbm.1), custom_call_target="tpu_custom_call" | custom-call | flops 8999999488 | bytes 11000000 | tf_op jit(solution)/shard_map/pallas_call | solution.py:578
  90.2 1.3 %copy.9 = f32[2,512]{1,0:T(2,128)} copy(f32[2,512]{1,0:T(2,128)} %shard_map.73) | data formatting | bytes 8192

commit v3 on v2

--- a/solution.py
+++ b/solution.py
@@ -89,9 +89,7 @@
         "dmy": V((3, 8, 128), F32),
         "dmc": V((8, 128), F32),
         "fcs": V((2, 8, 128), F32),
-        "fcr": V((8, 128), F32),
-        "fzs": V((8, 128), F32),
-        "fzr": V((7, 8, 128), F32),
+        "fzr": V((15, 8, 128), F32),
         "fps": V((8, 128), F32),
         "fpr": V((15, 8, 128), F32),
         "fin": V((2, 8, 128), F32),
@@ -184,25 +182,9 @@
         for dp, yy in ((d, yl),) + y_peers:
             if off or dp is not d or yy is not yl:
                 peers.append(dev(dp=dp, xx=xp(off), yy=yy))
-    peers.append(dev(ee=1 - e))
+    peers += [dev(z=zp(off), ee=1 - e) for off in range(NZ)]
     for peer in peers:
         pl.semaphore_signal(barrier, inc=1, device_id=peer, device_id_type=MESH)
-    right, left = dev(z=zp(1)), dev(z=zp(NZ - 1))
-
-    def along_z(distance, parts_right=(0, 1), parts_left=(0, 1)):
-        copies = []
-        for part in range(2):
-            if distance:
-                got(z_in[part])
-            if part in parts_right:
-                far = 4 if distance == 3 else -distance - 1
-                copies.append([send(place(-distance, part), place(far, part), right)])
-            else:
-                copies.append([])
-            if part in parts_left:
-                copies[-1].append(send(place(distance, part), place(distance + 1, part), left))
-        return copies
-
     partner = dev(ee=1 - e)
 
     def partial_group(tag, rows, lhs, h, q_group):
@@ -324,20 +306,20 @@
     s["qlt"][64:] = jnp.where(e == 0, turned[64:], turned[:64])
     get_qr.wait()
     s["qrt"][...] = s["qr"][...].astype(F32).T.astype(BF)
-    get_x.wait()
-    get_y.wait()
-    get_b.wait()
-    l_ready = [partial_group("l_", 64, s["qlt"], h, q) for h, q in groups[:2]]
     pl.semaphore_wait(barrier, len(peers))
 
-    z_in = along_z(0)
+    z_near = [
+        send(xg, place(-1), dev(z=zp(1))),
+        send(xg, place(1), dev(z=zp(NZ - 1))),
+        send(xg, place(-2), dev(z=zp(2))),
+    ]
+    z_far = [send(xg, place(2), dev(z=zp(NZ - 2)))]
     mine = s["y"].at[x * 2 + yl, e]
     y_in = []
     for off in range(NX):
         for yy in (yl, 1 - yl):
             if off or yy is not yl:
-                y_in.append(send(mine, mine, dev(xx=xp(off), yy=yy)))
-    l_core = [start() for start in l_ready]
+                y_in.append(send(yg, mine, dev(xx=xp(off), yy=yy)))
 
     def half_columns(half):
         return pl.ds(aligned(half * 256, 256), 256)
@@ -349,7 +331,8 @@
     factor_part = jnp.dot(s["qrt"][...], s["bin"][:, half_columns(d)], preferred_element_type=F32)
     s["ro"][...] = factor_part.reshape(8, 16, 256)
 
-    l_core += [partial_group("l_", 64, s["qlt"], h, q)() for h, q in groups[2:]]
+    get_b.wait()
+    l_core = [partial_group("l_", 64, s["qlt"], h, q)() for h, q in groups]
 
     def first_steps(tag, rows, core_copies, i):
         h, q_group = groups[i]
@@ -360,24 +343,10 @@
         return first_p(tag, rows, h, i)
 
     l_first = [first_steps("l_", 64, l_core, i) for i in range(4)]
-    z_in = along_z(1)
     got(y_in)
+    get_y.wait()
     y_half = s["y"].at[:, e]
     y_core = [send(y_half, y_half, partner)]
-
-    get_eig.wait()
-
-    def eig_sum(i, total):
-        rows = s["eig"][pl.ds(aligned(i * 128, 128), 128), :].astype(F32)
-        return total + jnp.sum(rows.reshape(16, 8, LB), axis=0)
-
-    total = lax.fori_loop(0, KH // 128, eig_sum, jnp.zeros((8, LB), F32))
-    s["dmp"][0] = total[:, :128] + total[:, 128:256] + total[:, 256:384] + total[:, 384:]
-    dm_z = [send(s["dmp"].at[0], s["dmz"].at[off - 1], dev(z=zp(off))) for off in range(1, NZ)]
-
-    got(r_dp)
-    s["ro"][...] += s["rr"][...]
-    r_z = [send(s["ro"].at[zp(off)], s["rzr"].at[off - 1], dev(z=zp(off))) for off in range(1, NZ)]
 
     got(y_core)
     token_part = jnp.dot(
@@ -390,27 +359,43 @@
     )
     s["ao"][...] = token_part.reshape(8, 64, 256)
 
-    z_in = along_z(2)
+    got(z_near)
+    z_next = [
+        send(place(-2), place(-3), dev(z=zp(1))),
+        send(place(-2, 0), place(4, 0), dev(z=zp(2))),
+    ]
+    got(z_far)
+    z_next += [
+        send(place(2), place(3), dev(z=zp(NZ - 1))),
+        send(place(2, 1), place(4, 1), dev(z=zp(NZ - 2))),
+    ]
+    get_x.wait()
 
     a_core, a_first_in = [], []
-    for i in range(2):
+    for i in range(4):
         a_core.append(partial_group("a_", ROWS, s["x"].at[0], *groups[i])())
-    a_first_in.append(first_steps("a_", ROWS, a_core, 0))
-    z_in = along_z(3, (0,), (1,))
-    for i in range(2, 4):
-        a_core.append(partial_group("a_", ROWS, s["x"].at[0], *groups[i])())
-        a_first_in.append(first_steps("a_", ROWS, a_core, i - 1))
+        if i:
+            a_first_in.append(first_steps("a_", ROWS, a_core, i - 1))
     a_first_in.append(first_steps("a_", ROWS, a_core, 3))
+    get_eig.wait()
+
+    def eig_sum(i, total):
+        rows = s["eig"][pl.ds(aligned(i * 128, 128), 128), :].astype(F32)
+        return total + jnp.sum(rows.reshape(16, 8, LB), axis=0)
+
+    total = lax.fori_loop(0, KH // 128, eig_sum, jnp.zeros((8, LB), F32))
+    s["dmp"][0] = total[:, :128] + total[:, 128:256] + total[:, 256:384] + total[:, 384:]
+    dm_z = [send(s["dmp"].at[0], s["dmz"].at[off - 1], dev(z=zp(off))) for off in range(1, NZ)]
+
+    got(r_dp)
+    s["ro"][...] += s["rr"][...]
+    r_z = [send(s["ro"].at[zp(off)], s["rzr"].at[off - 1], dev(z=zp(off))) for off in range(1, NZ)]
 
     got(a_dp)
     summed = s["ao"][...] + s["adr"][...].astype(F32)
     s["ao"][...] = summed
     s["azs"][...] = summed.astype(BF)
     a_z = [send(s["azs"].at[zp(off)], s["azr"].at[off - 1], dev(z=zp(off))) for off in range(1, NZ)]
-
-    got(dm_z)
-    s["dmp"][1] = s["dmp"][0] + jnp.sum(s["dmz"][...], axis=0)
-    dm_x = [send(s["dmp"].at[1], s["dmx"].at[off - 1], dev(xx=xp(off))) for off in range(1, NX)]
 
     def second_steps(tag, rows, first):
         got(first[0])
@@ -423,8 +408,7 @@
 
     l_second = second_steps("l_", 64, l_first)
 
-    got(z_in[0])
-    got(z_in[1])
+    got(z_next)
     b_core, b_first_in = [], []
     for i in range(4):
         b_core.append(partial_group("b_", ROWS, s["x"].at[1], *groups[i])())
@@ -432,22 +416,26 @@
             b_first_in.append(first_steps("b_", ROWS, b_core, i - 1))
     b_first_in.append(first_steps("b_", ROWS, b_core, 3))
 
+    got(dm_z)
+    s["dmp"][1] = s["dmp"][0] + jnp.sum(s["dmz"][...], axis=0)
+    dm_x = [send(s["dmp"].at[1], s["dmx"].at[off - 1], dev(xx=xp(off))) for off in range(1, NX)]
+
     got(r_z)
     factors = s["ro"][r] + jnp.sum(s["rzr"][...], axis=0)
     s["rfin"][d, r] = factors.astype(BF)
     mine = s["rfin"].at[d, r]
     r_f = [send(mine, mine, dev(z=zp(off))) for off in range(1, NZ)]
 
+    got(l_second)
+    l_f = last_sum("l_", 64)
+
+    a_second = second_steps("a_", ROWS, a_first_in)
+
     got(dm_x)
     s["dmp"][2] = s["dmp"][1] + jnp.sum(s["dmx"][...], axis=0)
     dm_y = [
         send(s["dmp"].at[2], s["dmy"].at[i], dev(dp=dp, yy=yy)) for i, (dp, yy) in enumerate(y_peers)
     ]
-
-    got(l_second)
-    l_f = last_sum("l_", 64)
-
-    a_second = second_steps("a_", ROWS, a_first_in)
 
     got(a_z)
     summed = s["ao"][r]
@@ -460,15 +448,15 @@
     got(r_f)
     mine = s["rfin"].at[d]
     r_last = [send(mine, mine, dev(dp=1 - d))]
+    got(l_f)
+    l_last = to_partner("l_", 64)
+
+    got(a_second)
+    a_out = last_sum("a_", ROWS)
+
     got(dm_y)
     s["dmp"][3] = s["dmp"][2] + jnp.sum(s["dmy"][...], axis=0)
     dm_c = [send(s["dmp"].at[3], s["dmc"], partner)]
-    got(l_f)
-    l_last = to_partner("l_", 64)
-
-    got(a_second)
-    a_out = last_sum("a_", ROWS)
-
     b_second = second_steps("b_", ROWS, b_first_in)
 
     got(dm_c)
@@ -496,12 +484,12 @@
 
     lax.fori_loop(0, KH // 128, precondition, 0)
 
+    got(b_second)
+    b_out = last_sum("b_", ROWS)
+
     got(a_f)
     mine = s["afin"].at[d]
     a_last = [send(mine, mine, dev(dp=1 - d))]
-
-    got(b_second)
-    b_out = last_sum("b_", ROWS)
 
     got(a_out)
     a_both = to_partner("a_", ROWS)
@@ -535,7 +523,7 @@
     got(a_both)
     score("a_", 0)
     drained = len(started)
-    for copy in started[: drained - 8]:
+    for copy in started[: drained - 9]:
         copy.wait_send()
     got(b_out)
     b_both = to_partner("b_", ROWS)
@@ -546,12 +534,13 @@
     for half in range(2):
         base = half * 256
         s["fcs"][half] = turned[:, base : base + 128] + turned[:, base + 128 : base + 256]
-    f_core = [send(s["fcs"].at[1 - e], s["fcr"], partner)]
-    got(f_core)
-    s["fzs"][...] = s["fcs"][e] + s["fcr"][...]
-    f_z = [send(s["fzs"], s["fzr"].at[off - 1], dev(z=zp(off))) for off in range(1, NZ)]
+    f_z = []
+    for off in range(NZ):
+        for ee in (e, 1 - e):
+            if off or ee is not e:
+                f_z.append(send(s["fcs"].at[ee], s["fzr"].at[len(f_z)], dev(z=zp(off), ee=ee)))
     got(f_z)
-    s["fps"][...] = s["fzs"][...] + jnp.sum(s["fzr"][...], axis=0)
+    s["fps"][...] = s["fcs"][e] + jnp.sum(s["fzr"][...], axis=0)
     f_plane = []
     for off in range(NX):
         for dp, yy in ((d, yl),) + y_peers:
@@ -569,7 +558,7 @@
             high = s["fin"][half, part * 4 + 2 : part * 4 + 4, :]
             out_ref[:, columns] = jnp.where(d == 0, low, high)
 
-    for copy in started[drained - 8 :]:
+    for copy in started[drained - 9 :]:
         copy.wait_send()
 
 

time: 91.6 us -> 90.4 us (0.987)
  Pallas kernels: 90.2 us -> 89 us
    pallas_call x1, Pallas kernels: 90.2 us -> 89 us  [local(): pl.pallas_call(kernel, out_shape=jax.ShapeDtypeStruct((2, TOK), F32), in_...]
where the time goes in v3:
time: 90.4 us; the launch traced here: 90.3 us
  Pallas kernels  89 us (98%)
  local copies, waits for them, and re-layouts  1.28 us (1%)
    pallas_call x1, Pallas kernels, local(): pl.pallas_call(kernel, out_shape=jax.ShapeDtypeStruct((2, TOK), F32), in_...  89 us

profile of v3, /device:TPU:1, one launch (start us, length us, event | category | flops | bytes accessed | tf_op | source)
XLA Modules:
  0.0 90.3 jit_solution(15726855196025254083)
XLA Ops:
  0.0 89.0 %shard_map.73 = f32[2,512]{1,0:T(2,128)} custom-call(bf16[64,896]{1,0:T(8,128)(2,1)} %xg.1, bf16[32,512]{1,0:T(8,128)(2,1)} %yg.1, bf16[896,3584]{1,0:T(8,128)(2,1)} %b_hbm.1, bf16[512,512]{1,0:T(8,128)(2,1)} %bin_hbm.1, bf16[3584,512]{1,0:T(8,128)(2,1)} %eig_hbm.1, bf16[896,128]{1,0:T(8,128)(2,1)} %ql_hbm.1, bf16[512,128]{1,0:T(8,128)(2,1)} %qr_hbm.1), custom_call_target="tpu_custom_call" | custom-call | flops 8999999488 | bytes 11000000 | tf_op jit(solution)/shard_map/pallas_call | solution.py:567
  89.0 1.3 %copy.9 = f32[2,512]{1,0:T(2,128)} copy(f32[2,512]{1,0:T(2,128)} %shard_map.73) | data formatting | bytes 8192

commit v4 on v3

--- a/solution.py
+++ b/solution.py
@@ -19,7 +19,7 @@
 IB = 896
 LB = 512
 JB = 512
-PW = 768
+PW = 1024
 QW = KH - PW
 TILE = 256
 ROWS = 128
@@ -70,13 +70,14 @@
         "rr": V((8, 16, 256), F32),
         "ro": V((8, 16, 256), F32),
         "rzr": V((7, 16, 256), F32),
-        "rfin": V((2, 8, 16, 256), BF),
-        "ads": V((8, 64, 256), BF),
-        "adr": V((8, 64, 256), BF),
-        "ao": V((8, 64, 256), F32),
-        "azs": V((8, 64, 256), BF),
-        "azr": V((7, 64, 256), BF),
-        "afin": V((2, 8, 64, 256), BF),
+        "rfin": V((8, 2, 16, 256), BF),
+        "ao": V((8, 64, LB), F32),
+        "azs": V((8, 64, LB), BF),
+        "azr": V((7, 64, LB), BF),
+        "ads": V((64, LB), BF),
+        "adr": V((64, LB), BF),
+        "asum": V((64, LB), F32),
+        "afin": V((8, 64, LB), BF),
         "rm": V((NQ, 128, LB), BF),
         "lt": V((KH, 128), BF),
         "pq": V((NQ, KH, LB), BF),
@@ -300,12 +301,6 @@
 
     groups = ((1 - d, True), (1 - d, False), (d, True), (d, False))
 
-    get_ql.wait()
-    turned = s["ql"][...].astype(F32).T.astype(BF)
-    s["qlt"][:64] = jnp.where(e == 0, turned[:64], turned[64:])
-    s["qlt"][64:] = jnp.where(e == 0, turned[64:], turned[:64])
-    get_qr.wait()
-    s["qrt"][...] = s["qr"][...].astype(F32).T.astype(BF)
     pl.semaphore_wait(barrier, len(peers))
 
     z_near = [
@@ -324,6 +319,12 @@
     def half_columns(half):
         return pl.ds(aligned(half * 256, 256), 256)
 
+    get_ql.wait()
+    turned = s["ql"][...].astype(F32).T.astype(BF)
+    s["qlt"][:64] = jnp.where(e == 0, turned[:64], turned[64:])
+    s["qlt"][64:] = jnp.where(e == 0, turned[64:], turned[:64])
+    get_qr.wait()
+    s["qrt"][...] = s["qr"][...].astype(F32).T.astype(BF)
     get_bin.wait()
     factor_part = jnp.dot(s["qrt"][...], s["bin"][:, half_columns(1 - d)], preferred_element_type=F32)
     s["rs"][...] = factor_part.reshape(8, 16, 256)
@@ -349,15 +350,10 @@
     y_core = [send(y_half, y_half, partner)]
 
     got(y_core)
-    token_part = jnp.dot(
-        s["y"][...].reshape(TOK, JB), s["bin"][:, half_columns(1 - d)], preferred_element_type=F32
-    )
-    s["ads"][...] = token_part.reshape(8, 64, 256).astype(BF)
-    a_dp = [send(s["ads"], s["adr"], dev(dp=1 - d))]
-    token_part = jnp.dot(
-        s["y"][...].reshape(TOK, JB), s["bin"][:, half_columns(d)], preferred_element_type=F32
-    )
-    s["ao"][...] = token_part.reshape(8, 64, 256)
+    token_part = jnp.dot(s["y"][...].reshape(TOK, JB), s["bin"][...], preferred_element_type=F32)
+    s["ao"][...] = token_part.reshape(8, 64, LB)
+    s["azs"][...] = token_part.reshape(8, 64, LB).astype(BF)
+    a_z = [send(s["azs"].at[zp(off)], s["azr"].at[off - 1], dev(z=zp(off))) for off in range(1, NZ)]
 
     got(z_near)
     z_next = [
@@ -391,12 +387,6 @@
     s["ro"][...] += s["rr"][...]
     r_z = [send(s["ro"].at[zp(off)], s["rzr"].at[off - 1], dev(z=zp(off))) for off in range(1, NZ)]
 
-    got(a_dp)
-    summed = s["ao"][...] + s["adr"][...].astype(F32)
-    s["ao"][...] = summed
-    s["azs"][...] = summed.astype(BF)
-    a_z = [send(s["azs"].at[zp(off)], s["azr"].at[off - 1], dev(z=zp(off))) for off in range(1, NZ)]
-
     def second_steps(tag, rows, first):
         got(first[0])
         got(first[2])
@@ -422,9 +412,17 @@
 
     got(r_z)
     factors = s["ro"][r] + jnp.sum(s["rzr"][...], axis=0)
-    s["rfin"][d, r] = factors.astype(BF)
-    mine = s["rfin"].at[d, r]
-    r_f = [send(mine, mine, dev(z=zp(off))) for off in range(1, NZ)]
+    s["rfin"][r, d] = factors.astype(BF)
+    mine = s["rfin"].at[r, d]
+    r_x = [send(mine, mine, dev(dp=1 - d))]
+
+    got(a_z)
+    summed = s["ao"][r]
+    for i in range(7):
+        summed += s["azr"][i].astype(F32)
+    s["asum"][...] = summed
+    s["ads"][...] = summed.astype(BF)
+    a_dp = [send(s["ads"], s["adr"], dev(dp=1 - d))]
 
     got(l_second)
     l_f = last_sum("l_", 64)
@@ -437,17 +435,13 @@
         send(s["dmp"].at[2], s["dmy"].at[i], dev(dp=dp, yy=yy)) for i, (dp, yy) in enumerate(y_peers)
     ]
 
-    got(a_z)
-    summed = s["ao"][r]
-    for i in range(7):
-        summed += s["azr"][i].astype(F32)
-    s["afin"][d, r] = summed.astype(BF)
-    mine = s["afin"].at[d, r]
+    got(r_x)
+    mine = s["rfin"].at[r]
+    r_f = [send(mine, mine, dev(z=zp(off))) for off in range(1, NZ)]
+    got(a_dp)
+    s["afin"][r] = (s["asum"][...] + s["adr"][...].astype(F32)).astype(BF)
+    mine = s["afin"].at[r]
     a_f = [send(mine, mine, dev(z=zp(off))) for off in range(1, NZ)]
-
-    got(r_f)
-    mine = s["rfin"].at[d]
-    r_last = [send(mine, mine, dev(dp=1 - d))]
     got(l_f)
     l_last = to_partner("l_", 64)
 
@@ -465,13 +459,13 @@
     for i in range(2):
         left_rows = s["l_f"][...].astype(F32)[:, i * 8 : (i + 1) * 8].reshape(128, KH // 2)
         s["lt"][i * (KH // 2) : (i + 1) * (KH // 2)] = left_rows.T.astype(BF)
-    got(r_last)
+    got(r_f)
     for q in range(NQ):
         s["rm"][q] = jnp.zeros((128, LB), BF)
         for g in range(2):
             rows = slice(q * RANK + g * 16, q * RANK + (g + 1) * 16)
             for half in range(2):
-                s["rm"][q, rows, half * 256 : (half + 1) * 256] = s["rfin"][half, q * 2 + g]
+                s["rm"][q, rows, half * 256 : (half + 1) * 256] = s["rfin"][q * 2 + g, half]
 
     def precondition(i, carry):
         rows = pl.ds(aligned(i * 128, 128), 128)
@@ -487,13 +481,9 @@
     got(b_second)
     b_out = last_sum("b_", ROWS)
 
-    got(a_f)
-    mine = s["afin"].at[d]
-    a_last = [send(mine, mine, dev(dp=1 - d))]
-
     got(a_out)
     a_both = to_partner("a_", ROWS)
-    got(a_last)
+    got(a_f)
 
     lanes = lax.broadcasted_iota(jnp.int32, (2 * ROWS, 128), 1)
     block_of = lax.broadcasted_iota(jnp.int32, (2 * ROWS, 128), 0) // 64
@@ -503,9 +493,7 @@
         odd = jnp.zeros_like(lanes)
         for j, block in enumerate(blocks):
             odd = jnp.where(block_of == j, lax.rem(block // 2, 2), odd)
-            for half in range(2):
-                columns = slice(half * 256, (half + 1) * 256)
-                s["at"][j * 64 : (j + 1) * 64, columns] = s["afin"][half, block].astype(F32)
+            s["at"][j * 64 : (j + 1) * 64] = s["afin"][block].astype(F32)
         s["mc"][...] = jnp.zeros((2 * ROWS, 128), F32)
 
         def one_query(q, carry):
@@ -523,7 +511,7 @@
     got(a_both)
     score("a_", 0)
     drained = len(started)
-    for copy in started[: drained - 9]:
+    for copy in started[: drained - 8]:
         copy.wait_send()
     got(b_out)
     b_both = to_partner("b_", ROWS)
@@ -558,7 +546,7 @@
             high = s["fin"][half, part * 4 + 2 : part * 4 + 4, :]
             out_ref[:, columns] = jnp.where(d == 0, low, high)
 
-    for copy in started[drained - 9 :]:
+    for copy in started[drained - 8 :]:
         copy.wait_send()
 
 

time: 90.4 us -> 91.1 us (level)
  no operation moved by 1% of the time
where the time goes in v4:
time: 91.1 us; the launch traced here: 90.9 us
  Pallas kernels  89.7 us (98%)
  local copies, waits for them, and re-layouts  1.28 us (1%)
    pallas_call x1, Pallas kernels, local(): pl.pallas_call(kernel, out_shape=jax.ShapeDtypeStruct((2, TOK), F32), in_...  89.7 us

profile of v4, /device:TPU:1, one launch (start us, length us, event | category | flops | bytes accessed | tf_op | source)
XLA Modules:
  0.0 90.9 jit_solution(16123264677059351721)
XLA Ops:
  0.0 89.7 %shard_map.73 = f32[2,512]{1,0:T(2,128)} custom-call(bf16[64,896]{1,0:T(8,128)(2,1)} %xg.1, bf16[32,512]{1,0:T(8,128)(2,1)} %yg.1, bf16[896,3584]{1,0:T(8,128)(2,1)} %b_hbm.1, bf16[512,512]{1,0:T(8,128)(2,1)} %bin_hbm.1, bf16[3584,512]{1,0:T(8,128)(2,1)} %eig_hbm.1, bf16[896,128]{1,0:T(8,128)(2,1)} %ql_hbm.1, bf16[512,128]{1,0:T(8,128)(2,1)} %qr_hbm.1), custom_call_target="tpu_custom_call" | custom-call | flops 8999999488 | bytes 11000000 | tf_op jit(solution)/shard_map/pallas_call | solution.py:555
  89.7 1.3 %copy.9 = f32[2,512]{1,0:T(2,128)} copy(f32[2,512]{1,0:T(2,128)} %shard_map.73) | data formatting | bytes 8192

commit v5 on v4

--- a/solution.py
+++ b/solution.py
@@ -71,17 +71,17 @@
         "ro": V((8, 16, 256), F32),
         "rzr": V((7, 16, 256), F32),
         "rfin": V((8, 2, 16, 256), BF),
-        "ao": V((8, 64, LB), F32),
-        "azs": V((8, 64, LB), BF),
-        "azr": V((7, 64, LB), BF),
-        "ads": V((64, LB), BF),
-        "adr": V((64, LB), BF),
-        "asum": V((64, LB), F32),
-        "afin": V((8, 64, LB), BF),
+        "ao": V((8, 64, 256), F32),
+        "azs": V((8, 64, 256), BF),
+        "azr": V((7, 64, 256), BF),
+        "ads": V((8, 64, 256), BF),
+        "adr": V((8, 64, 256), BF),
+        "afin": V((8, 2, 64, 256), BF),
         "rm": V((NQ, 128, LB), BF),
         "lt": V((KH, 128), BF),
         "pq": V((NQ, KH, LB), BF),
         "at": V((2 * ROWS, LB), F32),
+        "sv": V((2, NQ, 2 * ROWS, LB), F32),
         "mc": V((2 * ROWS, 128), F32),
         "m": V((TOK, 128), F32),
         "dmp": V((4, 8, 128), F32),
@@ -343,17 +343,23 @@
             return first_q(tag, (0, 1) if i == 0 else (2,))
         return first_p(tag, rows, h, i)
 
-    l_first = [first_steps("l_", 64, l_core, i) for i in range(4)]
     got(y_in)
     get_y.wait()
     y_half = s["y"].at[:, e]
     y_core = [send(y_half, y_half, partner)]
 
     got(y_core)
-    token_part = jnp.dot(s["y"][...].reshape(TOK, JB), s["bin"][...], preferred_element_type=F32)
-    s["ao"][...] = token_part.reshape(8, 64, LB)
-    s["azs"][...] = token_part.reshape(8, 64, LB).astype(BF)
-    a_z = [send(s["azs"].at[zp(off)], s["azr"].at[off - 1], dev(z=zp(off))) for off in range(1, NZ)]
+    def input_part(half):
+        part = jnp.dot(
+            s["y"][...].reshape(TOK, JB), s["bin"][:, half_columns(half)], preferred_element_type=F32
+        )
+        return part.reshape(8, 64, 256)
+
+    s["ads"][...] = input_part(1 - d).astype(BF)
+    a_dp = [send(s["ads"], s["adr"], dev(dp=1 - d))]
+    s["ao"][...] = input_part(d)
+
+    l_first = [first_steps("l_", 64, l_core, i) for i in range(4)]
 
     got(z_near)
     z_next = [
@@ -373,6 +379,12 @@
         if i:
             a_first_in.append(first_steps("a_", ROWS, a_core, i - 1))
     a_first_in.append(first_steps("a_", ROWS, a_core, 3))
+    got(a_dp)
+    summed = s["ao"][...] + s["adr"][...].astype(F32)
+    s["ao"][...] = summed
+    s["azs"][...] = summed.astype(BF)
+    a_z = [send(s["azs"].at[zp(off)], s["azr"].at[off - 1], dev(z=zp(off))) for off in range(1, NZ)]
+
     get_eig.wait()
 
     def eig_sum(i, total):
@@ -416,14 +428,6 @@
     mine = s["rfin"].at[r, d]
     r_x = [send(mine, mine, dev(dp=1 - d))]
 
-    got(a_z)
-    summed = s["ao"][r]
-    for i in range(7):
-        summed += s["azr"][i].astype(F32)
-    s["asum"][...] = summed
-    s["ads"][...] = summed.astype(BF)
-    a_dp = [send(s["ads"], s["adr"], dev(dp=1 - d))]
-
     got(l_second)
     l_f = last_sum("l_", 64)
 
@@ -435,13 +439,17 @@
         send(s["dmp"].at[2], s["dmy"].at[i], dev(dp=dp, yy=yy)) for i, (dp, yy) in enumerate(y_peers)
     ]
 
+    got(a_z)
+    summed = s["ao"][r]
+    for i in range(7):
+        summed += s["azr"][i].astype(F32)
+    s["afin"][r, d] = summed.astype(BF)
+    mine = s["afin"].at[r, d]
+    a_x = [send(mine, mine, dev(dp=1 - d))]
+
     got(r_x)
     mine = s["rfin"].at[r]
     r_f = [send(mine, mine, dev(z=zp(off))) for off in range(1, NZ)]
-    got(a_dp)
-    s["afin"][r] = (s["asum"][...] + s["adr"][...].astype(F32)).astype(BF)
-    mine = s["afin"].at[r]
-    a_f = [send(mine, mine, dev(z=zp(off))) for off in range(1, NZ)]
     got(l_f)
     l_last = to_partner("l_", 64)
 
@@ -451,6 +459,9 @@
     got(dm_y)
     s["dmp"][3] = s["dmp"][2] + jnp.sum(s["dmy"][...], axis=0)
     dm_c = [send(s["dmp"].at[3], s["dmc"], partner)]
+    got(a_x)
+    mine = s["afin"].at[r]
+    a_f = [send(mine, mine, dev(z=zp(off))) for off in range(1, NZ)]
     b_second = second_steps("b_", ROWS, b_first_in)
 
     got(dm_c)
@@ -483,22 +494,29 @@
 
     got(a_out)
     a_both = to_partner("a_", ROWS)
-    got(a_f)
 
     lanes = lax.broadcasted_iota(jnp.int32, (2 * ROWS, 128), 1)
     block_of = lax.broadcasted_iota(jnp.int32, (2 * ROWS, 128), 0) // 64
 
-    def score(tag, chunk):
+    def weigh(tag, chunk):
+        def one_query(q, carry):
+            s["sv"][chunk, q] = jnp.dot(s[tag + "f"][...], s["pq"][q], preferred_element_type=F32)
+            return carry
+
+        lax.fori_loop(0, NQ, one_query, 0)
+
+    def score(chunk):
         blocks = [lax.rem(r + ORDER[chunk * 4 + j] + NZ, NZ) for j in range(4)]
         odd = jnp.zeros_like(lanes)
         for j, block in enumerate(blocks):
             odd = jnp.where(block_of == j, lax.rem(block // 2, 2), odd)
-            s["at"][j * 64 : (j + 1) * 64] = s["afin"][block].astype(F32)
+            for half in range(2):
+                columns = slice(half * 256, (half + 1) * 256)
+                s["at"][j * 64 : (j + 1) * 64, columns] = s["afin"][block, half].astype(F32)
         s["mc"][...] = jnp.zeros((2 * ROWS, 128), F32)
 
         def one_query(q, carry):
-            weighted = jnp.dot(s[tag + "f"][...], s["pq"][q], preferred_element_type=F32)
-            terms = weighted * s["at"][...]
+            terms = s["sv"][chunk, q] * s["at"][...]
             total = terms[:, :128] + terms[:, 128:256] + terms[:, 256:384] + terms[:, 384:]
             scores = jnp.sum(total, axis=1, keepdims=True)
             s["mc"][...] += jnp.where(lanes == q + 4 * odd, scores, 0.0)
@@ -509,14 +527,17 @@
             s["m"][pl.ds(aligned(block * 64, 64), 64), :] = s["mc"][j * 64 : (j + 1) * 64, :]
 
     got(a_both)
-    score("a_", 0)
-    drained = len(started)
-    for copy in started[: drained - 8]:
-        copy.wait_send()
+    weigh("a_", 0)
     got(b_out)
     b_both = to_partner("b_", ROWS)
+    drained = len(started)
+    for copy in started[: drained - 9]:
+        copy.wait_send()
     got(b_both)
-    score("b_", 1)
+    weigh("b_", 1)
+    got(a_f)
+    score(0)
+    score(1)
 
     turned = s["m"][...].T[:8]
     for half in range(2):
@@ -546,7 +567,7 @@
             high = s["fin"][half, part * 4 + 2 : part * 4 + 4, :]
             out_ref[:, columns] = jnp.where(d == 0, low, high)
 
-    for copy in started[drained - 8 :]:
+    for copy in started[drained - 9 :]:
         copy.wait_send()
 
 

time: 91.1 us -> 84.7 us (0.930)
  Pallas kernels: 89.7 us -> 83.3 us
    pallas_call x1, Pallas kernels: 89.7 us -> 83.3 us  [local(): pl.pallas_call(kernel, out_shape=jax.ShapeDtypeStruct((2, TOK), F32), in_...]
where the time goes in v5:
time: 84.7 us; the launch traced here: 84.6 us
  Pallas kernels  83.3 us (98%)
  local copies, waits for them, and re-layouts  1.28 us (2%)
    pallas_call x1, Pallas kernels, local(): pl.pallas_call(kernel, out_shape=jax.ShapeDtypeStruct((2, TOK), F32), in_...  83.3 us

profile of v5, /device:TPU:1, one launch (start us, length us, event | category | flops | bytes accessed | tf_op | source)
XLA Modules:
  0.0 84.6 jit_solution(2007571197349957188)
XLA Ops:
  0.0 83.3 %shard_map.73 = f32[2,512]{1,0:T(2,128)} custom-call(bf16[64,896]{1,0:T(8,128)(2,1)} %xg.1, bf16[32,512]{1,0:T(8,128)(2,1)} %yg.1, bf16[896,3584]{1,0:T(8,128)(2,1)} %b_hbm.1, bf16[512,512]{1,0:T(8,128)(2,1)} %bin_hbm.1, bf16[3584,512]{1,0:T(8,128)(2,1)} %eig_hbm.1, bf16[896,128]{1,0:T(8,128)(2,1)} %ql_hbm.1, bf16[512,128]{1,0:T(8,128)(2,1)} %qr_hbm.1), custom_call_target="tpu_custom_call" | custom-call | flops 8999999488 | bytes 11000000 | tf_op jit(solution)/shard_map/pallas_call | solution.py:576
  83.3 1.3 %copy.9 = f32[2,512]{1,0:T(2,128)} copy(f32[2,512]{1,0:T(2,128)} %shard_map.73) | data formatting | bytes 8192

commit v6 on v5

--- a/solution.py
+++ b/solution.py
@@ -101,7 +101,8 @@
     return shapes
 
 
-N_SEM = 176
+N_SEND = 64
+N_RECV = 70
 NAMES = tuple(scratch())
 
 
@@ -132,21 +133,42 @@
     y_peers = ((1 - d, yl), (1 - d, 1 - yl), (d, 1 - yl))
 
     started = []
+    settled = []
+    landings = []
     local_started = []
 
-    def send(src, dst, device):
-        k = len(started)
-        copy = pltpu.make_async_remote_copy(
+    def describe(src, dst, device, send_index, landing):
+        return pltpu.make_async_remote_copy(
             src_ref=src,
             dst_ref=dst,
-            send_sem=send_sems.at[k],
-            recv_sem=recv_sems.at[k],
+            send_sem=send_sems.at[send_index],
+            recv_sem=recv_sems.at[landing],
             device_id=device,
             device_id_type=MESH,
         )
+
+    def settle(count):
+        while len(settled) < count:
+            started[len(settled)].wait_send()
+            settled.append(True)
+
+    def start(src, dst, device, landing):
+        settle(len(started) - N_SEND + 1)
+        copy = describe(src, dst, device, len(started) % N_SEND, landing)
         copy.start()
         started.append(copy)
         return copy
+
+    def send(src, dst, device):
+        landings.append(True)
+        return start(src, dst, device, len(landings) - 1)
+
+    def together(extent, copies):
+        landings.append(True)
+        landing = len(landings) - 1
+        for src, dst, device in copies:
+            start(src, dst, device, landing)
+        return [describe(extent, extent, dev(ee=1 - e), 0, landing)]
 
     def fetch(src, dst):
         copy = pltpu.make_async_copy(src, dst, local_sems.at[len(local_started)])
@@ -225,21 +247,24 @@
 
     def first_p(tag, rows, h, slot_h):
         quarter = rows // 4
-        return [
-            send(
+        copies = [
+            (
                 s[tag + "ps"].at[h, pl.ds(aligned(xp(off) * quarter, quarter), quarter)],
                 s[tag + "pr"].at[h, off - 1],
                 dev(xx=xp(off)),
             )
             for off in range(1, NX)
         ]
+        return together(s[tag + "pr"].at[h], copies)
 
     def first_q(tag, which):
-        return [
-            send(s[tag + "qs"].at[dp, yy], s[tag + "qr"].at[i], dev(dp=dp, yy=yy))
+        landing = s[tag + "qr"]
+        copies = [
+            (s[tag + "qs"].at[dp, yy], landing.at[i], dev(dp=dp, yy=yy))
             for i, (dp, yy) in enumerate(y_peers)
             if i in which
         ]
+        return together(landing.at[pl.ds(which[0], len(which))], copies)
 
     def second_p(tag, rows, h, which):
         eighth, quarter = rows // 8, rows // 4
@@ -250,11 +275,13 @@
                 total += s[tag + "pr"][h, i, yy * eighth : (yy + 1) * eighth, :].astype(F32)
             s[tag + "p2f"][h, yy] = total
             s[tag + "p2"][h, yy] = total.astype(s[tag + "p2"].dtype)
-        return [
-            send(s[tag + "p2"].at[dp, yy], s[tag + "pr2"].at[i], dev(dp=dp, yy=yy))
+        landing = s[tag + "pr2"]
+        copies = [
+            (s[tag + "p2"].at[dp, yy], landing.at[i], dev(dp=dp, yy=yy))
             for i, (dp, yy) in enumerate(y_peers)
             if i in which
         ]
+        return together(landing.at[pl.ds(which[0], len(which))], copies)
 
     def second_q(tag, rows):
         eighth, quarter = rows // 8, rows // 4
@@ -265,10 +292,11 @@
                 total += s[tag + "qr"][i, xx].astype(F32)
             s[tag + "q2f"][xx] = total
             s[tag + "q2"][xx] = total.astype(s[tag + "q2"].dtype)
-        return [
-            send(s[tag + "q2"].at[xp(off)], s[tag + "qr2"].at[off - 1], dev(xx=xp(off)))
+        copies = [
+            (s[tag + "q2"].at[xp(off)], s[tag + "qr2"].at[off - 1], dev(xx=xp(off)))
             for off in range(1, NX)
         ]
+        return together(s[tag + "qr2"], copies)
 
     def last_sum(tag, rows):
         eighth, quarter = rows // 8, rows // 4
@@ -291,8 +319,8 @@
         for off in range(NX):
             for yy in (yl, 1 - yl):
                 if off or yy is not yl:
-                    copies.append(send(block, block, dev(xx=xp(off), yy=yy)))
-        return copies
+                    copies.append((block, block, dev(xx=xp(off), yy=yy)))
+        return together(s[tag + "f"].at[pl.ds(0, 7 * eighth if rows >= 128 else 7)], copies)
 
     def to_partner(tag, rows):
         count = rows if rows >= 128 else 8
@@ -303,18 +331,35 @@
 
     pl.semaphore_wait(barrier, len(peers))
 
-    z_near = [
-        send(xg, place(-1), dev(z=zp(1))),
-        send(xg, place(1), dev(z=zp(NZ - 1))),
-        send(xg, place(-2), dev(z=zp(2))),
+    right, left = dev(z=zp(1)), dev(z=zp(NZ - 1))
+
+    def own_half(part):
+        return xg.at[pl.ds(part * 32, 32)]
+
+    z_in = [
+        [send(own_half(part), place(-1, part), right), send(own_half(part), place(1, part), left)]
+        for part in range(2)
     ]
-    z_far = [send(xg, place(2), dev(z=zp(NZ - 2)))]
+
+    def along_z(distance, arrived):
+        copies = []
+        for part in range(2):
+            got(arrived[part])
+            copies.append([])
+            if distance < 3 or part == 0:
+                far = 4 if distance == 3 else -distance - 1
+                copies[part].append(send(place(-distance, part), place(far, part), right))
+            if distance < 3 or part == 1:
+                copies[part].append(send(place(distance, part), place(distance + 1, part), left))
+        return copies
+
     mine = s["y"].at[x * 2 + yl, e]
     y_in = []
     for off in range(NX):
         for yy in (yl, 1 - yl):
             if off or yy is not yl:
-                y_in.append(send(yg, mine, dev(xx=xp(off), yy=yy)))
+                y_in.append((yg, mine, dev(xx=xp(off), yy=yy)))
+    y_in = together(s["y"].at[pl.ds(0, 7), 0], y_in)
 
     def half_columns(half):
         return pl.ds(aligned(half * 256, 256), 256)
@@ -333,7 +378,9 @@
     s["ro"][...] = factor_part.reshape(8, 16, 256)
 
     get_b.wait()
-    l_core = [partial_group("l_", 64, s["qlt"], h, q)() for h, q in groups]
+    l_core = [partial_group("l_", 64, s["qlt"], h, q)() for h, q in groups[:2]]
+    z_in = along_z(1, z_in)
+    l_core += [partial_group("l_", 64, s["qlt"], h, q)() for h, q in groups[2:]]
 
     def first_steps(tag, rows, core_copies, i):
         h, q_group = groups[i]
@@ -359,31 +406,23 @@
     a_dp = [send(s["ads"], s["adr"], dev(dp=1 - d))]
     s["ao"][...] = input_part(d)
 
+    z_in = along_z(2, z_in)
+    get_x.wait()
     l_first = [first_steps("l_", 64, l_core, i) for i in range(4)]
-
-    got(z_near)
-    z_next = [
-        send(place(-2), place(-3), dev(z=zp(1))),
-        send(place(-2, 0), place(4, 0), dev(z=zp(2))),
-    ]
-    got(z_far)
-    z_next += [
-        send(place(2), place(3), dev(z=zp(NZ - 1))),
-        send(place(2, 1), place(4, 1), dev(z=zp(NZ - 2))),
-    ]
-    get_x.wait()
 
     a_core, a_first_in = [], []
     for i in range(4):
         a_core.append(partial_group("a_", ROWS, s["x"].at[0], *groups[i])())
         if i:
             a_first_in.append(first_steps("a_", ROWS, a_core, i - 1))
+        if i == 1:
+            z_in = along_z(3, z_in)
     a_first_in.append(first_steps("a_", ROWS, a_core, 3))
     got(a_dp)
     summed = s["ao"][...] + s["adr"][...].astype(F32)
     s["ao"][...] = summed
     s["azs"][...] = summed.astype(BF)
-    a_z = [send(s["azs"].at[zp(off)], s["azr"].at[off - 1], dev(z=zp(off))) for off in range(1, NZ)]
+    a_z = together(s["azr"], [(s["azs"].at[zp(off)], s["azr"].at[off - 1], dev(z=zp(off))) for off in range(1, NZ)])
 
     get_eig.wait()
 
@@ -393,11 +432,11 @@
 
     total = lax.fori_loop(0, KH // 128, eig_sum, jnp.zeros((8, LB), F32))
     s["dmp"][0] = total[:, :128] + total[:, 128:256] + total[:, 256:384] + total[:, 384:]
-    dm_z = [send(s["dmp"].at[0], s["dmz"].at[off - 1], dev(z=zp(off))) for off in range(1, NZ)]
+    dm_z = together(s["dmz"], [(s["dmp"].at[0], s["dmz"].at[off - 1], dev(z=zp(off))) for off in range(1, NZ)])
 
     got(r_dp)
     s["ro"][...] += s["rr"][...]
-    r_z = [send(s["ro"].at[zp(off)], s["rzr"].at[off - 1], dev(z=zp(off))) for off in range(1, NZ)]
+    r_z = together(s["rzr"], [(s["ro"].at[zp(off)], s["rzr"].at[off - 1], dev(z=zp(off))) for off in range(1, NZ)])
 
     def second_steps(tag, rows, first):
         got(first[0])
@@ -410,7 +449,7 @@
 
     l_second = second_steps("l_", 64, l_first)
 
-    got(z_next)
+    got(z_in[0] + z_in[1])
     b_core, b_first_in = [], []
     for i in range(4):
         b_core.append(partial_group("b_", ROWS, s["x"].at[1], *groups[i])())
@@ -420,7 +459,7 @@
 
     got(dm_z)
     s["dmp"][1] = s["dmp"][0] + jnp.sum(s["dmz"][...], axis=0)
-    dm_x = [send(s["dmp"].at[1], s["dmx"].at[off - 1], dev(xx=xp(off))) for off in range(1, NX)]
+    dm_x = together(s["dmx"], [(s["dmp"].at[1], s["dmx"].at[off - 1], dev(xx=xp(off))) for off in range(1, NX)])
 
     got(r_z)
     factors = s["ro"][r] + jnp.sum(s["rzr"][...], axis=0)
@@ -435,9 +474,10 @@
 
     got(dm_x)
     s["dmp"][2] = s["dmp"][1] + jnp.sum(s["dmx"][...], axis=0)
-    dm_y = [
-        send(s["dmp"].at[2], s["dmy"].at[i], dev(dp=dp, yy=yy)) for i, (dp, yy) in enumerate(y_peers)
-    ]
+    dm_y = together(
+        s["dmy"],
+        [(s["dmp"].at[2], s["dmy"].at[i], dev(dp=dp, yy=yy)) for i, (dp, yy) in enumerate(y_peers)],
+    )
 
     got(a_z)
     summed = s["ao"][r]
@@ -449,7 +489,7 @@
 
     got(r_x)
     mine = s["rfin"].at[r]
-    r_f = [send(mine, mine, dev(z=zp(off))) for off in range(1, NZ)]
+    r_f = together(s["rfin"].at[pl.ds(0, 7)], [(mine, mine, dev(z=zp(off))) for off in range(1, NZ)])
     got(l_f)
     l_last = to_partner("l_", 64)
 
@@ -461,7 +501,7 @@
     dm_c = [send(s["dmp"].at[3], s["dmc"], partner)]
     got(a_x)
     mine = s["afin"].at[r]
-    a_f = [send(mine, mine, dev(z=zp(off))) for off in range(1, NZ)]
+    a_f = together(s["afin"].at[pl.ds(0, 7)], [(mine, mine, dev(z=zp(off))) for off in range(1, NZ)])
     b_second = second_steps("b_", ROWS, b_first_in)
 
     got(dm_c)
@@ -530,9 +570,7 @@
     weigh("a_", 0)
     got(b_out)
     b_both = to_partner("b_", ROWS)
-    drained = len(started)
-    for copy in started[: drained - 9]:
-        copy.wait_send()
+    settle(len(started) - 9)
     got(b_both)
     weigh("b_", 1)
     got(a_f)
@@ -547,15 +585,15 @@
     for off in range(NZ):
         for ee in (e, 1 - e):
             if off or ee is not e:
-                f_z.append(send(s["fcs"].at[ee], s["fzr"].at[len(f_z)], dev(z=zp(off), ee=ee)))
-    got(f_z)
+                f_z.append((s["fcs"].at[ee], s["fzr"].at[len(f_z)], dev(z=zp(off), ee=ee)))
+    got(together(s["fzr"], f_z))
     s["fps"][...] = s["fcs"][e] + jnp.sum(s["fzr"][...], axis=0)
     f_plane = []
     for off in range(NX):
         for dp, yy in ((d, yl),) + y_peers:
             if off or dp is not d or yy is not yl:
-                f_plane.append(send(s["fps"], s["fpr"].at[len(f_plane)], dev(dp=dp, xx=xp(off), yy=yy)))
-    got(f_plane)
+                f_plane.append((s["fps"], s["fpr"].at[len(f_plane)], dev(dp=dp, xx=xp(off), yy=yy)))
+    got(together(s["fpr"], f_plane))
     s["fin"][e] = s["fps"][...] + jnp.sum(s["fpr"][...], axis=0)
     mine = s["fin"].at[e]
     f_last = [send(mine, mine, partner)]
@@ -567,8 +605,8 @@
             high = s["fin"][half, part * 4 + 2 : part * 4 + 4, :]
             out_ref[:, columns] = jnp.where(d == 0, low, high)
 
-    for copy in started[drained - 9 :]:
-        copy.wait_send()
+    settle(len(started))
+    assert len(landings) <= N_RECV
 
 
 def local(out_grads, layer_inputs, basis_output, basis_input, eigenvalues, query_left, query_right):
@@ -580,8 +618,8 @@
         out_specs=pl.BlockSpec(memory_space=pltpu.VMEM),
         scratch_shapes=list(scratch().values())
         + [
-            pltpu.SemaphoreType.DMA((N_SEM,)),
-            pltpu.SemaphoreType.DMA((N_SEM,)),
+            pltpu.SemaphoreType.DMA((N_SEND,)),
+            pltpu.SemaphoreType.DMA((N_RECV,)),
             pltpu.SemaphoreType.DMA((8,)),
         ],
         compiler_params=pltpu.CompilerParams(

time: 84.7 us -> 82.5 us (0.974)
  Pallas kernels: 83.3 us -> 81.1 us
    pallas_call x1, Pallas kernels: 83.3 us -> 81.1 us  [local(): pl.pallas_call(kernel, out_shape=jax.ShapeDtypeStruct((2, TOK), F32), in_...]
where the time goes in v6:
time: 82.5 us; the launch traced here: 82.4 us
  Pallas kernels  81.1 us (98%)
  local copies, waits for them, and re-layouts  1.28 us (2%)
    pallas_call x1, Pallas kernels, local(): pl.pallas_call(kernel, out_shape=jax.ShapeDtypeStruct((2, TOK), F32), in_...  81.1 us

profile of v6, /device:TPU:1, one launch (start us, length us, event | category | flops | bytes accessed | tf_op | source)
XLA Modules:
  0.0 82.4 jit_solution(258656134949775466)
XLA Ops:
  0.0 81.1 %shard_map.73 = f32[2,512]{1,0:T(2,128)} custom-call(bf16[64,896]{1,0:T(8,128)(2,1)} %xg.1, bf16[32,512]{1,0:T(8,128)(2,1)} %yg.1, bf16[896,3584]{1,0:T(8,128)(2,1)} %b_hbm.1, bf16[512,512]{1,0:T(8,128)(2,1)} %bin_hbm.1, bf16[3584,512]{1,0:T(8,128)(2,1)} %eig_hbm.1, bf16[896,128]{1,0:T(8,128)(2,1)} %ql_hbm.1, bf16[512,128]{1,0:T(8,128)(2,1)} %qr_hbm.1), custom_call_target="tpu_custom_call" | custom-call | flops 8999999488 | bytes 11000000 | tf_op jit(solution)/shard_map/pallas_call | solution.py:614
  81.1 1.3 %copy.9 = f32[2,512]{1,0:T(2,128)} copy(f32[2,512]{1,0:T(2,128)} %shard_map.73) | data formatting | bytes 8192

commit v7 on v6

--- a/solution.py
+++ b/solution.py
@@ -406,6 +406,16 @@
     a_dp = [send(s["ads"], s["adr"], dev(dp=1 - d))]
     s["ao"][...] = input_part(d)
 
+    get_eig.wait()
+
+    def eig_sum(i, total):
+        rows = s["eig"][pl.ds(aligned(i * 128, 128), 128), :].astype(F32)
+        return total + jnp.sum(rows.reshape(16, 8, LB), axis=0)
+
+    total = lax.fori_loop(0, KH // 128, eig_sum, jnp.zeros((8, LB), F32))
+    s["dmp"][0] = total[:, :128] + total[:, 128:256] + total[:, 256:384] + total[:, 384:]
+    dm_z = together(s["dmz"], [(s["dmp"].at[0], s["dmz"].at[off - 1], dev(z=zp(off))) for off in range(1, NZ)])
+
     z_in = along_z(2, z_in)
     get_x.wait()
     l_first = [first_steps("l_", 64, l_core, i) for i in range(4)]
@@ -417,26 +427,15 @@
             a_first_in.append(first_steps("a_", ROWS, a_core, i - 1))
         if i == 1:
             z_in = along_z(3, z_in)
+            got(r_dp)
+            s["ro"][...] += s["rr"][...]
+            r_z = together(s["rzr"], [(s["ro"].at[zp(off)], s["rzr"].at[off - 1], dev(z=zp(off))) for off in range(1, NZ)])
     a_first_in.append(first_steps("a_", ROWS, a_core, 3))
     got(a_dp)
     summed = s["ao"][...] + s["adr"][...].astype(F32)
     s["ao"][...] = summed
     s["azs"][...] = summed.astype(BF)
     a_z = together(s["azr"], [(s["azs"].at[zp(off)], s["azr"].at[off - 1], dev(z=zp(off))) for off in range(1, NZ)])
-
-    get_eig.wait()
-
-    def eig_sum(i, total):
-        rows = s["eig"][pl.ds(aligned(i * 128, 128), 128), :].astype(F32)
-        return total + jnp.sum(rows.reshape(16, 8, LB), axis=0)
-
-    total = lax.fori_loop(0, KH // 128, eig_sum, jnp.zeros((8, LB), F32))
-    s["dmp"][0] = total[:, :128] + total[:, 128:256] + total[:, 256:384] + total[:, 384:]
-    dm_z = together(s["dmz"], [(s["dmp"].at[0], s["dmz"].at[off - 1], dev(z=zp(off))) for off in range(1, NZ)])
-
-    got(r_dp)
-    s["ro"][...] += s["rr"][...]
-    r_z = together(s["rzr"], [(s["ro"].at[zp(off)], s["rzr"].at[off - 1], dev(z=zp(off))) for off in range(1, NZ)])
 
     def second_steps(tag, rows, first):
         got(first[0])
@@ -447,8 +446,6 @@
         got(first[3])
         return copies + second_p(tag, rows, d, (2,))
 
-    l_second = second_steps("l_", 64, l_first)
-
     got(z_in[0] + z_in[1])
     b_core, b_first_in = [], []
     for i in range(4):
@@ -457,6 +454,8 @@
             b_first_in.append(first_steps("b_", ROWS, b_core, i - 1))
     b_first_in.append(first_steps("b_", ROWS, b_core, 3))
 
+    a_second = second_steps("a_", ROWS, a_first_in)
+
     got(dm_z)
     s["dmp"][1] = s["dmp"][0] + jnp.sum(s["dmz"][...], axis=0)
     dm_x = together(s["dmx"], [(s["dmp"].at[1], s["dmx"].at[off - 1], dev(xx=xp(off))) for off in range(1, NX)])
@@ -467,17 +466,7 @@
     mine = s["rfin"].at[r, d]
     r_x = [send(mine, mine, dev(dp=1 - d))]
 
-    got(l_second)
-    l_f = last_sum("l_", 64)
-
-    a_second = second_steps("a_", ROWS, a_first_in)
-
-    got(dm_x)
-    s["dmp"][2] = s["dmp"][1] + jnp.sum(s["dmx"][...], axis=0)
-    dm_y = together(
-        s["dmy"],
-        [(s["dmp"].at[2], s["dmy"].at[i], dev(dp=dp, yy=yy)) for i, (dp, yy) in enumerate(y_peers)],
-    )
+    l_second = second_steps("l_", 64, l_first)
 
     got(a_z)
     summed = s["ao"][r]
@@ -490,20 +479,30 @@
     got(r_x)
     mine = s["rfin"].at[r]
     r_f = together(s["rfin"].at[pl.ds(0, 7)], [(mine, mine, dev(z=zp(off))) for off in range(1, NZ)])
-    got(l_f)
-    l_last = to_partner("l_", 64)
+
+    got(dm_x)
+    s["dmp"][2] = s["dmp"][1] + jnp.sum(s["dmx"][...], axis=0)
+    dm_y = together(
+        s["dmy"],
+        [(s["dmp"].at[2], s["dmy"].at[i], dev(dp=dp, yy=yy)) for i, (dp, yy) in enumerate(y_peers)],
+    )
+
+    got(l_second)
+    l_f = last_sum("l_", 64)
 
     got(a_second)
     a_out = last_sum("a_", ROWS)
 
+    got(a_x)
+    mine = s["afin"].at[r]
+    a_f = together(s["afin"].at[pl.ds(0, 7)], [(mine, mine, dev(z=zp(off))) for off in range(1, NZ)])
     got(dm_y)
     s["dmp"][3] = s["dmp"][2] + jnp.sum(s["dmy"][...], axis=0)
     dm_c = [send(s["dmp"].at[3], s["dmc"], partner)]
-    got(a_x)
-    mine = s["afin"].at[r]
-    a_f = together(s["afin"].at[pl.ds(0, 7)], [(mine, mine, dev(z=zp(off))) for off in range(1, NZ)])
     b_second = second_steps("b_", ROWS, b_first_in)
 
+    got(l_f)
+    l_last = to_partner("l_", 64)
     got(dm_c)
     damping = jnp.sum(s["dmp"][3] + s["dmc"][...], keepdims=True) * (DAMP_RATIO / (DG * DA))
     got(l_last)

time: 82.5 us -> 84.5 us (1.024)
  Pallas kernels: 81.1 us -> 83.1 us
    pallas_call x1, Pallas kernels: 81.1 us -> 83.1 us  [local(): pl.pallas_call(kernel, out_shape=jax.ShapeDtypeStruct((2, TOK), F32), in_...]
where the time goes in v7:
time: 84.5 us; the launch traced here: 84.4 us
  Pallas kernels  83.1 us (98%)
  local copies, waits for them, and re-layouts  1.28 us (2%)
    pallas_call x1, Pallas kernels, local(): pl.pallas_call(kernel, out_shape=jax.ShapeDtypeStruct((2, TOK), F32), in_...  83.1 us

profile of v7, /device:TPU:1, one launch (start us, length us, event | category | flops | bytes accessed | tf_op | source)
XLA Modules:
  0.0 84.4 jit_solution(7276973301187917037)
XLA Ops:
  0.0 83.1 %shard_map.73 = f32[2,512]{1,0:T(2,128)} custom-call(bf16[64,896]{1,0:T(8,128)(2,1)} %xg.1, bf16[32,512]{1,0:T(8,128)(2,1)} %yg.1, bf16[896,3584]{1,0:T(8,128)(2,1)} %b_hbm.1, bf16[512,512]{1,0:T(8,128)(2,1)} %bin_hbm.1, bf16[3584,512]{1,0:T(8,128)(2,1)} %eig_hbm.1, bf16[896,128]{1,0:T(8,128)(2,1)} %ql_hbm.1, bf16[512,128]{1,0:T(8,128)(2,1)} %qr_hbm.1), custom_call_target="tpu_custom_call" | custom-call | flops 8999999488 | bytes 11000000 | tf_op jit(solution)/shard_map/pallas_call | solution.py:613
  83.1 1.3 %copy.9 = f32[2,512]{1,0:T(2,128)} copy(f32[2,512]{1,0:T(2,128)} %shard_map.73) | data formatting | bytes 8192
